TPU v7x, 512 devices: a whole 4x8x8 slice. The times are simulated.
512 devices in a mesh: dp: 16 (over x_lo, z), seq: 32 (over y, x_hi, core).
Axes of the slice: x: 4 (x_hi: 2, x_lo: 2; x = x_hi * 2 + x_lo), y: 8, z: 8, core: 2. Of those that a mesh axis runs over, the one named last changes fastest.
Arguments:
- query_input: bfloat16 [65536, 4096], P(('dp', 'seq')), may hold values from -6 to 6
- key_input: bfloat16 [65536, 512], P(('dp', 'seq')), may hold values from -6 to 6
- value_input: bfloat16 [65536, 512], P(('dp', 'seq')), may hold values from -6 to 6
- output_gradient: bfloat16 [65536, 4096], P(('dp', 'seq')), may hold values from -6 to 6
Outputs:
- grad_query: bfloat16 [65536, 4096], P(('dp', 'seq'))
- grad_key: bfloat16 [65536, 512], P(('dp', 'seq'))
- grad_value: bfloat16 [65536, 512], P(('dp', 'seq'))
- query_bias_gradient: float32 [32, 128], P('seq')
- keyvalue_bias_gradient: float32 [2, 512], replicated
All inputs are finite; a program needn't handle non-finite values.
Results may differ from a plain program's by a relative error of at most 0.0079.
Values may be sent and summed in bfloat16 or wider, within the bound.
A program may use at most 128 MiB of HBM per device.

v0:
```python
import math

import jax
import jax.numpy as jnp
from jax import lax
from jax.sharding import PartitionSpec as P

QUERY_HEADS = 32
KEYVALUE_HEADS = 4
HEAD_SIZE = 128
SEQS = 2


def spread_heads(lookup_table, replica_count):
    count_of_rows = lookup_table.shape[0]
    gathered_heads = lookup_table.reshape(count_of_rows, KEYVALUE_HEADS, 1, HEAD_SIZE)
    return jnp.broadcast_to(
        gathered_heads, (count_of_rows, KEYVALUE_HEADS, replica_count, HEAD_SIZE)
    ).reshape(count_of_rows, KEYVALUE_HEADS * replica_count * HEAD_SIZE)


def block_grads(query_row_block, gradient_rows, key_row_block, value_row_block, offset, scaling):
    scores = (
        jnp.einsum(
            "bhd,kd->hbk", query_row_block, key_row_block, preferred_element_type=jnp.float32
        )
        * scaling
    )
    row_ids = lax.broadcasted_iota(jnp.int32, scores.shape, 1) + offset
    col_ids = lax.broadcasted_iota(jnp.int32, scores.shape, 2)
    scores = jnp.where(col_ids <= row_ids, scores, -jnp.inf)
    peak = jnp.max(scores, axis=2, keepdims=True)
    log_total = peak + jnp.log(jnp.sum(jnp.exp(scores - peak), axis=2, keepdims=True))
    probs = jnp.exp(scores - log_total)
    probs_half = probs.astype(jnp.bfloat16)
    output = jnp.einsum(
        "hbk,kd->bhd", probs_half, value_row_block, preferred_element_type=jnp.float32
    )
    delta = jnp.sum(gradient_rows.astype(jnp.float32) * output, axis=2)
    value_gradient_total = jnp.einsum(
        "hbk,bhd->kd", probs_half, gradient_rows, preferred_element_type=jnp.float32
    )
    dprobs = jnp.einsum(
        "bhd,kd->hbk", gradient_rows, value_row_block, preferred_element_type=jnp.float32
    )
    dscores = (probs * (dprobs - delta.T[:, :, None]) * scaling).astype(jnp.bfloat16)
    query_grad = jnp.einsum(
        "hbk,kd->bhd", dscores, key_row_block, preferred_element_type=jnp.float32
    )
    key_gradient_total = jnp.einsum(
        "hbk,bhd->kd", dscores, query_row_block, preferred_element_type=jnp.float32
    )
    return (query_grad, key_gradient_total, value_gradient_total)


def local(query_input, key_input, value_input, output_gradient):
    token_rows = query_input.shape[0]
    sequence_workers = lax.axis_size("seq")
    data_devices = lax.axis_size("dp")
    replica_count = sequence_workers // KEYVALUE_HEADS
    per_dev = QUERY_HEADS // sequence_workers
    span_length = token_rows * sequence_workers
    seq_len = span_length // SEQS
    block_count = max(1, seq_len // 256)
    width = seq_len // block_count
    scaling = 1.0 / math.sqrt(HEAD_SIZE)
    root_norm = 1.0 / math.sqrt(span_length * data_devices)
    head_query, head_grad, head_key, head_value = (
        lax.all_to_all(query_input, "seq", split_axis=1, concat_axis=0, tiled=True),
        lax.all_to_all(output_gradient, "seq", split_axis=1, concat_axis=0, tiled=True),
        lax.all_to_all(
            spread_heads(key_input, replica_count), "seq", split_axis=1, concat_axis=0, tiled=True
        ),
        lax.all_to_all(
            spread_heads(value_input, replica_count), "seq", split_axis=1, concat_axis=0, tiled=True
        ),
    )
    key_total = jnp.zeros((span_length, HEAD_SIZE), jnp.float32)
    value_total = jnp.zeros((span_length, HEAD_SIZE), jnp.float32)
    query_parts = []
    for seq_index in range(SEQS):
        seq_start = seq_index * seq_len
        for block_index in range(block_count):
            row_start = seq_start + block_index * width
            row_end = row_start + width
            query_row_block = head_query[row_start:row_end].reshape(width, per_dev, HEAD_SIZE)
            gradient_rows = head_grad[row_start:row_end].reshape(width, per_dev, HEAD_SIZE)
            key_row_block = head_key[seq_start:row_end]
            value_row_block = head_value[seq_start:row_end]
            query_grad, key_gradient_total, value_gradient_total = block_grads(
                query_row_block,
                gradient_rows,
                key_row_block,
                value_row_block,
                block_index * width,
                scaling,
            )
            query_parts.append(query_grad.reshape(width, per_dev * HEAD_SIZE))
            key_total = key_total.at[seq_start:row_end].add(key_gradient_total)
            value_total = value_total.at[seq_start:row_end].add(value_gradient_total)
    query_full = jnp.concatenate(query_parts, axis=0)
    grad_query = lax.all_to_all(
        query_full.astype(jnp.bfloat16), "seq", split_axis=0, concat_axis=1, tiled=True
    )
    query_sum = jnp.sum(query_full, axis=0)
    query_bias_gradient = lax.psum(query_sum, "dp").reshape(per_dev, HEAD_SIZE) * root_norm
    received_key, received_value = (
        lax.all_to_all(key_total, "seq", split_axis=0, concat_axis=1, tiled=True),
        lax.all_to_all(value_total, "seq", split_axis=0, concat_axis=1, tiled=True),
    )
    key_sequence = jnp.sum(
        received_key.reshape(token_rows, KEYVALUE_HEADS, replica_count, HEAD_SIZE), axis=2
    ).reshape(token_rows, KEYVALUE_HEADS * HEAD_SIZE)
    value_sequence = jnp.sum(
        received_value.reshape(token_rows, KEYVALUE_HEADS, replica_count, HEAD_SIZE), axis=2
    ).reshape(token_rows, KEYVALUE_HEADS * HEAD_SIZE)
    local_sums = jnp.stack([jnp.sum(key_sequence, axis=0), jnp.sum(value_sequence, axis=0)])
    keyvalue_bias_gradient = lax.psum(local_sums, ("dp", "seq")) * root_norm
    return (
        grad_query,
        key_sequence.astype(jnp.bfloat16),
        value_sequence.astype(jnp.bfloat16),
        query_bias_gradient,
        keyvalue_bias_gradient,
    )


def solution(mesh):
    in_specs = (
        P(("dp", "seq"), None),
        P(("dp", "seq"), None),
        P(("dp", "seq"), None),
        P(("dp", "seq"), None),
    )
    out_specs = (
        P(("dp", "seq"), None),
        P(("dp", "seq"), None),
        P(("dp", "seq"), None),
        P("seq", None),
        P(),
    )
    return jax.shard_map(local, mesh=mesh, in_specs=in_specs, out_specs=out_specs, check_vma=False)
```

profile of v0, /device:TPU:1, one launch (start us, length us, event | category | flops | bytes accessed | tf_op | source)
XLA Modules:
  0.0 549.1 jit_solution(16368588227525010026)
XLA Ops:
  2.8 11.2 %all-to-all-start = ((bf16[128,32,128]{2,0,1:T(8,128)(2,1)}), bf16[128,32,128]{2,0,1:T(8,128)(2,1)S(1)}, u32[]{:S(2)}, u32[]{:S(2)}) async-start(bf16[128,32,128]{2,0,1:T(8,128)(2,1)} %bitcast), calls=%async_computation | async-start | bytes 2097152 | tf_op jit(solution)/shard_map/all_to_all | solution.py:71
  14.1 28.1 %all-to-all-done = bf16[128,32,128]{2,0,1:T(8,128)(2,1)S(1)} async-done(((bf16[128,32,128]{2,0,1:T(8,128)(2,1)}), bf16[128,32,128]{2,0,1:T(8,128)(2,1)S(1)}, u32[]{:S(2)}, u32[]{:S(2)}) %all-to-all-start) | async-done | bytes 1048608 | tf_op jit(solution)/shard_map/all_to_all | solution.py:71
  43.4 5.8 %all-to-all-start.2 = ((bf16[128,32,128]{2,0,1:T(8,128)(2,1)}), bf16[128,32,128]{2,0,1:T(8,128)(2,1)S(1)}, u32[]{:S(2)}, u32[]{:S(2)}) async-start(bf16[128,32,128]{2,0,1:T(8,128)(2,1)} %bitcast.8), calls=%async_computation.2 | async-start | bytes 2097152 | tf_op jit(solution)/shard_map/all_to_all | solution.py:74
  52.2 25.1 %all-to-all-done.2 = bf16[128,32,128]{2,0,1:T(8,128)(2,1)S(1)} async-done(((bf16[128,32,128]{2,0,1:T(8,128)(2,1)}), bf16[128,32,128]{2,0,1:T(8,128)(2,1)S(1)}, u32[]{:S(2)}, u32[]{:S(2)}) %all-to-all-start.2) | async-done | bytes 1048608 | tf_op jit(solution)/shard_map/all_to_all | solution.py:74
  77.3 5.8 %all-to-all-start.1 = ((bf16[128,32,128]{0,2,1:T(8,128)(2,1)}), bf16[128,32,128]{0,2,1:T(8,128)(2,1)S(1)}, u32[]{:S(2)}, u32[]{:S(2)}) async-start(bf16[128,32,128]{0,2,1:T(8,128)(2,1)} %bitcast.1076), calls=%async_computation.1 | async-start | bytes 2097152 | tf_op jit(solution)/shard_map/all_to_all | solution.py:69
  83.7 2.3 copy.119
  92.1 19.1 %all-to-all-done.1 = bf16[128,32,128]{0,2,1:T(8,128)(2,1)S(1)} async-done(((bf16[128,32,128]{0,2,1:T(8,128)(2,1)}), bf16[128,32,128]{0,2,1:T(8,128)(2,1)S(1)}, u32[]{:S(2)}, u32[]{:S(2)}) %all-to-all-start.1) | async-done | bytes 1048608 | tf_op jit(solution)/shard_map/all_to_all | solution.py:69
  112.2 5.8 %all-to-all-start.3 = ((bf16[128,32,128]{0,2,1:T(8,128)(2,1)}), bf16[128,32,128]{0,2,1:T(8,128)(2,1)S(1)}, u32[]{:S(2)}, u32[]{:S(2)}) async-start(bf16[128,32,128]{0,2,1:T(8,128)(2,1)} %bitcast.11), calls=%async_computation.3 | async-start | bytes 2097152 | tf_op jit(solution)/shard_map/all_to_all | solution.py:70
  118.0 2.2 fusion.255
  128.3 17.9 %all-to-all-done.3 = bf16[128,32,128]{0,2,1:T(8,128)(2,1)S(1)} async-done(((bf16[128,32,128]{0,2,1:T(8,128)(2,1)}), bf16[128,32,128]{0,2,1:T(8,128)(2,1)S(1)}, u32[]{:S(2)}, u32[]{:S(2)}) %all-to-all-start.3) | async-done | bytes 1048608 | tf_op jit(solution)/shard_map/all_to_all | solution.py:70
  188.7 1.6 copy.158
  190.4 2.1 fusion.141
  193.9 1.8 fusion.146
  196.4 1.7 copy.159
  198.1 2.4 fusion.135
  201.8 1.7 fusion.132
  203.4 1.7 copy.160
  205.1 2.6 fusion.117
  212.6 2.8 fusion.55
  217.0 1.6 copy.162
  218.7 3.1 fusion.59
  224.7 1.6 copy.163
  226.4 3.3 fusion.63
  231.8 1.6 copy.164
  233.4 3.5 fusion.77
  241.3 1.8 fusion.168
  245.6 1.6 copy.166
  250.5 1.7 copy.168
  253.7 1.7 copy.169
  255.4 1.7 copy.170
  258.7 1.7 copy.171
  260.3 1.6 copy.172
  292.1 5.8 %all-to-all-start.4 = ((bf16[32,128,128]{2,1,0:T(8,128)(2,1)}), bf16[32,128,128]{2,1,0:T(8,128)(2,1)}, u32[]{:S(2)}, u32[]{:S(2)}) async-start(bf16[32,128,128]{2,1,0:T(8,128)(2,1)} %bitcast.1114), calls=%async_computation.4 | async-start | bytes 2097152 | tf_op jit(solution)/shard_map/all_to_all | solution.py:102
  298.0 2.2 fusion.140
  300.2 2.3 fusion.134
  302.5 2.2 fusion.116
  304.7 2.4 fusion.54
  307.1 2.6 fusion.58
  309.7 2.6 fusion.62
  312.3 2.7 fusion.76
  315.0 11.2 %all-to-all-done.4 = bf16[32,128,128]{2,1,0:T(8,128)(2,1)} async-done(((bf16[32,128,128]{2,1,0:T(8,128)(2,1)}), bf16[32,128,128]{2,1,0:T(8,128)(2,1)}, u32[]{:S(2)}, u32[]{:S(2)}) %all-to-all-start.4) | async-done | bytes 1048608 | tf_op jit(solution)/shard_map/all_to_all | solution.py:102
  326.2 5.9 %all-to-all-start.6 = ((f32[32,128,128]{2,1,0:T(8,128)}), f32[32,128,128]{2,1,0:T(8,128)S(1)}, u32[]{:S(2)}, u32[]{:S(2)}) async-start(f32[32,128,128]{2,1,0:T(8,128)} %bitcast.238), calls=%async_computation.6 | async-start | bytes 4194304 | tf_op jit(solution)/shard_map/all_to_all | solution.py:109
  333.2 2.0 fusion.137
  335.2 2.2 fusion.119
  337.5 2.4 fusion.57
  339.8 2.4 fusion.61
  342.3 2.7 fusion.65
  345.0 2.7 fusion.79
  347.7 1.8 fusion.169
  349.5 1.9 fusion.142
  351.5 2.0 fusion.136
  353.5 2.2 fusion.118
  355.7 2.3 fusion.56
  358.1 2.4 fusion.60
  360.5 2.6 fusion.64
  363.1 2.6 fusion.78
  365.7 16.5 %all-to-all-done.6 = f32[32,128,128]{2,1,0:T(8,128)S(1)} async-done(((f32[32,128,128]{2,1,0:T(8,128)}), f32[32,128,128]{2,1,0:T(8,128)S(1)}, u32[]{:S(2)}, u32[]{:S(2)}) %all-to-all-start.6) | async-done | bytes 2097184 | tf_op jit(solution)/shard_map/all_to_all | solution.py:109
  382.3 6.6 %all-to-all-start.5 = ((f32[32,128,128]{2,1,0:T(8,128)}), f32[32,128,128]{2,1,0:T(8,128)}, u32[]{:S(2)}, u32[]{:S(2)}) async-start(f32[32,128,128]{2,1,0:T(8,128)} %bitcast.234), calls=%async_computation.5 | async-start | bytes 4194304 | tf_op jit(solution)/shard_map/all_to_all | solution.py:108
  394.2 35.7 %psum.14 = f32[128]{0:T(128)S(1)} all-reduce(f32[128]{0:T(128)S(1)} %add_add_fusion), channel_id=1, replica_groups=mesh['dp'=16,'seq'=32] {'dp'}, use_global_device_ids=true, to_apply=%region_66.67 | all-reduce | flops 128 | bytes 1024 | tf_op jit(solution)/shard_map/psum | solution.py:106
  430.5 2.3 copy_bitcast_fusion
  433.0 6.0 %all-to-all-done.5 = f32[32,128,128]{2,1,0:T(8,128)} async-done(((f32[32,128,128]{2,1,0:T(8,128)}), f32[32,128,128]{2,1,0:T(8,128)}, u32[]{:S(2)}, u32[]{:S(2)}) %all-to-all-start.5) | async-done | bytes 2097184 | tf_op jit(solution)/shard_map/all_to_all | solution.py:108
  439.0 1.7 bitcast_reduce_fusion.3
  440.7 103.9 %psum.15 = f32[2,512]{1,0:T(2,128)S(1)} all-reduce(f32[2,512]{1,0:T(2,128)S(1)} %pad_maximum_fusion), channel_id=1, replica_groups=mesh['dp'=16,'seq'=32] {'dp','seq'}, use_global_device_ids=true, to_apply=%region_71.72 | all-reduce | flops 1024 | bytes 8192 | tf_op jit(solution)/shard_map/psum | solution.py:118
  546.2 1.7 bitcast_reduce_fusion.1
  (627 shorter events, 131.5 us)
Async XLA Ops:
  0.6 13.4 %copy-start.200 = (bf16[128,512]{1,0:T(8,128)(2,1)S(1)}, bf16[128,512]{1,0:T(8,128)(2,1)}, u32[]{:S(2)}) copy-start(bf16[128,512]{1,0:T(8,128)(2,1)} %param.70) | copy-start | bytes 393220
  2.8 39.4 %all-to-all-start = ((bf16[128,32,128]{2,0,1:T(8,128)(2,1)}), bf16[128,32,128]{2,0,1:T(8,128)(2,1)S(1)}, u32[]{:S(2)}, u32[]{:S(2)}) async-start(bf16[128,32,128]{2,0,1:T(8,128)(2,1)} %bitcast), calls=%async_computation | async-start | bytes 2097152 | tf_op jit(solution)/shard_map/all_to_all | solution.py:71
  14.0 35.1 %copy-start.111 = (bf16[128,4096]{1,0:T(8,128)(2,1)S(1)}, bf16[128,4096]{1,0:T(8,128)(2,1)}, u32[]{:S(2)}) copy-start(bf16[128,4096]{1,0:T(8,128)(2,1)} %param.68) | copy-start | bytes 3145732
  43.4 33.9 %all-to-all-start.2 = ((bf16[128,32,128]{2,0,1:T(8,128)(2,1)}), bf16[128,32,128]{2,0,1:T(8,128)(2,1)S(1)}, u32[]{:S(2)}, u32[]{:S(2)}) async-start(bf16[128,32,128]{2,0,1:T(8,128)(2,1)} %bitcast.8), calls=%async_computation.2 | async-start | bytes 2097152 | tf_op jit(solution)/shard_map/all_to_all | solution.py:74
  52.2 106.3 %copy-start.216 = (s32[256]{0:T(256)}, s32[256]{0:T(256)S(1)}, u32[]{:S(2)}) copy-start(s32[256]{0:T(256)S(1)} %iota_add_fusion.3) | copy-start | bytes 3076
  52.2 108.2 %copy-start.214 = (s32[256]{0:T(256)}, s32[256]{0:T(256)S(1)}, u32[]{:S(2)}) copy-start(s32[256]{0:T(256)S(1)} %iota_add_fusion.2) | copy-start | bytes 3076
  77.3 33.9 %all-to-all-start.1 = ((bf16[128,32,128]{0,2,1:T(8,128)(2,1)}), bf16[128,32,128]{0,2,1:T(8,128)(2,1)S(1)}, u32[]{:S(2)}, u32[]{:S(2)}) async-start(bf16[128,32,128]{0,2,1:T(8,128)(2,1)} %bitcast.1076), calls=%async_computation.1 | async-start | bytes 2097152 | tf_op jit(solution)/shard_map/all_to_all | solution.py:69
  85.9 79.4 %copy-start.212 = (s32[256]{0:T(256)}, s32[256]{0:T(256)S(1)}, u32[]{:S(2)}) copy-start(s32[256]{0:T(256)S(1)} %iota_add_fusion) | copy-start | bytes 3076
  86.6 33.8 %copy-start.129 = (bf16[2,128,128]{2,1,0:T(8,128)(2,1)}, bf16[2,128,128]{2,1,0:T(8,128)(2,1)S(1)}, u32[]{:S(2)}) copy-start(bf16[2,128,128]{2,1,0:T(8,128)(2,1)S(1)} %get-tuple-element.460) | copy-start | bytes 196612
  112.2 33.9 %all-to-all-start.3 = ((bf16[128,32,128]{0,2,1:T(8,128)(2,1)}), bf16[128,32,128]{0,2,1:T(8,128)(2,1)S(1)}, u32[]{:S(2)}, u32[]{:S(2)}) async-start(bf16[128,32,128]{0,2,1:T(8,128)(2,1)} %bitcast.11), calls=%async_computation.3 | async-start | bytes 2097152 | tf_op jit(solution)/shard_map/all_to_all | solution.py:70
  149.1 5.1 copy-start.121
  149.1 5.1 copy-start.219
  150.6 5.5 %copy-start.193 = (bf16[2,128,128]{1,2,0:T(8,128)(2,1)S(1)}, bf16[2,128,128]{1,2,0:T(8,128)(2,1)}, u32[]{:S(2)}) copy-start(bf16[2,128,128]{1,2,0:T(8,128)(2,1)} %get-tuple-element.411) | copy-start | bytes 196612
  151.5 4.7 copy-start.115
  151.5 4.7 copy-start.218
  151.6 5.0 copy-start.196
  167.8 4.6 copy-start.119
  169.9 4.7 copy-start.113
  190.4 5.3 copy-start.106
  190.4 5.3 copy-start.109
  192.5 5.6 %copy-start.110 = (bf16[2,128,128]{2,1,0:T(8,128)(2,1)S(1)}, bf16[2,128,128]{2,1,0:T(8,128)(2,1)}, u32[]{:S(2)}) copy-start(bf16[2,128,128]{2,1,0:T(8,128)(2,1)} %get-tuple-element.430) | copy-start | bytes 196612
  198.1 7.1 %copy-start.107 = (bf16[2,128,128]{2,1,0:T(8,128)(2,1)S(1)}, bf16[2,128,128]{2,1,0:T(8,128)(2,1)}, u32[]{:S(2)}) copy-start(bf16[2,128,128]{2,1,0:T(8,128)(2,1)} %get-tuple-element.429) | copy-start | bytes 196612
  244.4 17.6 %copy-start.204 = (f32[256]{0:T(256)S(1)}, f32[256]{0:T(256)}, u32[]{:S(2)}) copy-start(f32[256]{0:T(256)} %log_add_fusion.6) | copy-start | bytes 3076
  265.0 18.8 %copy-start.62 = (bf16[256,512]{0,1:T(8,128)(2,1)}, bf16[256,512]{0,1:T(8,128)(2,1)S(1)}, u32[]{:S(2)}) copy-start(bf16[256,512]{0,1:T(8,128)(2,1)S(1)} %fusion.147) | copy-start | bytes 786436
  267.0 17.8 %copy-start.58 = (bf16[256,768]{0,1:T(8,128)(2,1)}, bf16[256,768]{0,1:T(8,128)(2,1)S(1)}, u32[]{:S(2)}) copy-start(bf16[256,768]{0,1:T(8,128)(2,1)S(1)} %fusion.133) | copy-start | bytes 1179652
  267.7 18.0 %copy-start.47 = (bf16[256,1024]{0,1:T(8,128)(2,1)}, bf16[256,1024]{0,1:T(8,128)(2,1)S(1)}, u32[]{:S(2)}) copy-start(bf16[256,1024]{0,1:T(8,128)(2,1)S(1)} %fusion.113) | copy-start | bytes 1572868
  268.9 17.9 %copy-start.43 = (bf16[256,1280]{0,1:T(8,128)(2,1)}, bf16[256,1280]{0,1:T(8,128)(2,1)S(1)}, u32[]{:S(2)}) copy-start(bf16[256,1280]{0,1:T(8,128)(2,1)S(1)} %fusion.68) | copy-start | bytes 1966084
  270.5 17.3 %copy-start.38 = (bf16[256,1536]{0,1:T(8,128)(2,1)}, bf16[256,1536]{0,1:T(8,128)(2,1)S(1)}, u32[]{:S(2)}) copy-start(bf16[256,1536]{0,1:T(8,128)(2,1)S(1)} %fusion.72) | copy-start | bytes 2359300
  272.9 16.0 %copy-start.34 = (bf16[256,1792]{0,1:T(8,128)(2,1)}, bf16[256,1792]{0,1:T(8,128)(2,1)S(1)}, u32[]{:S(2)}) copy-start(bf16[256,1792]{0,1:T(8,128)(2,1)S(1)} %fusion.75) | copy-start | bytes 2752516
  274.6 15.5 %copy-start.27 = (bf16[256,2048]{0,1:T(8,128)(2,1)}, bf16[256,2048]{0,1:T(8,128)(2,1)S(1)}, u32[]{:S(2)}) copy-start(bf16[256,2048]{0,1:T(8,128)(2,1)S(1)} %fusion.71) | copy-start | bytes 3145732
  274.6 4.9 copy-start.36
  274.6 4.9 copy-start.80
  281.7 5.0 copy-start.82
  292.1 34.0 %all-to-all-start.4 = ((bf16[32,128,128]{2,1,0:T(8,128)(2,1)}), bf16[32,128,128]{2,1,0:T(8,128)(2,1)}, u32[]{:S(2)}, u32[]{:S(2)}) async-start(bf16[32,128,128]{2,1,0:T(8,128)(2,1)} %bitcast.1114), calls=%async_computation.4 | async-start | bytes 2097152 | tf_op jit(solution)/shard_map/all_to_all | solution.py:102
  326.2 6.0 %copy-start.65 = (bf16[256,512]{0,1:T(8,128)(2,1)S(1)}, bf16[256,512]{0,1:T(8,128)(2,1)}, u32[]{:S(2)}) copy-start(bf16[256,512]{0,1:T(8,128)(2,1)} %fusion.146) | copy-start | bytes 786436
  326.2 6.0 %copy-start.88 = (f32[256,128]{1,0:T(8,128)S(1)}, f32[256,128]{1,0:T(8,128)}, u32[]{:S(2)}) copy-start(f32[256,128]{1,0:T(8,128)} %fusion.289) | copy-start | bytes 393220
  326.2 6.0 %copy-start.197 = (bf16[2,128,128]{2,1,0:T(8,128)(2,1)S(1)}, bf16[2,128,128]{2,1,0:T(8,128)(2,1)}, u32[]{:S(2)}) copy-start(bf16[2,128,128]{2,1,0:T(8,128)(2,1)} %copy-done.196) | copy-start | bytes 196612
  326.2 7.0 %copy-start.57 = (bf16[256,768]{0,1:T(8,128)(2,1)S(1)}, bf16[256,768]{0,1:T(8,128)(2,1)}, u32[]{:S(2)}) copy-start(bf16[256,768]{0,1:T(8,128)(2,1)} %fusion.132) | copy-start | bytes 1179652
  326.2 7.0 %copy-start.159 = (bf16[2,128,128]{2,1,0:T(8,128)(2,1)S(1)}, bf16[2,128,128]{2,1,0:T(8,128)(2,1)}, u32[]{:S(2)}) copy-start(bf16[2,128,128]{2,1,0:T(8,128)(2,1)} %copy-done.158) | copy-start | bytes 196612
  326.2 56.0 %all-to-all-start.6 = ((f32[32,128,128]{2,1,0:T(8,128)}), f32[32,128,128]{2,1,0:T(8,128)S(1)}, u32[]{:S(2)}, u32[]{:S(2)}) async-start(f32[32,128,128]{2,1,0:T(8,128)} %bitcast.238), calls=%async_computation.6 | async-start | bytes 4194304 | tf_op jit(solution)/shard_map/all_to_all | solution.py:109
  332.2 5.3 copy-start.42
  332.2 5.2 copy-start.163
  337.4 4.8 copy-start.33
  337.4 4.8 copy-start.167
  345.0 6.5 %copy-start.59 = (bf16[256,768]{0,1:T(8,128)(2,1)S(1)}, bf16[256,768]{0,1:T(8,128)(2,1)}, u32[]{:S(2)}) copy-start(bf16[256,768]{0,1:T(8,128)(2,1)} %copy-done.58) | copy-start | bytes 1179652
  345.0 6.5 %copy-start.171 = (bf16[2,128,128]{2,1,0:T(8,128)(2,1)S(1)}, bf16[2,128,128]{2,1,0:T(8,128)(2,1)}, u32[]{:S(2)}) copy-start(bf16[2,128,128]{2,1,0:T(8,128)(2,1)} %copy-done.170) | copy-start | bytes 196612
  347.7 5.8 %copy-start.48 = (bf16[256,1024]{0,1:T(8,128)(2,1)S(1)}, bf16[256,1024]{0,1:T(8,128)(2,1)}, u32[]{:S(2)}) copy-start(bf16[256,1024]{0,1:T(8,128)(2,1)} %copy-done.47) | copy-start | bytes 1572868
  347.7 5.8 %copy-start.173 = (bf16[2,128,128]{2,1,0:T(8,128)(2,1)S(1)}, bf16[2,128,128]{2,1,0:T(8,128)(2,1)}, u32[]{:S(2)}) copy-start(bf16[2,128,128]{2,1,0:T(8,128)(2,1)} %copy-done.172) | copy-start | bytes 196612
  349.5 6.2 %copy-start.44 = (bf16[256,1280]{0,1:T(8,128)(2,1)S(1)}, bf16[256,1280]{0,1:T(8,128)(2,1)}, u32[]{:S(2)}) copy-start(bf16[256,1280]{0,1:T(8,128)(2,1)} %copy-done.43) | copy-start | bytes 1966084
  349.5 6.2 %copy-start.175 = (bf16[2,128,128]{2,1,0:T(8,128)(2,1)S(1)}, bf16[2,128,128]{2,1,0:T(8,128)(2,1)}, u32[]{:S(2)}) copy-start(bf16[2,128,128]{2,1,0:T(8,128)(2,1)} %copy-done.174) | copy-start | bytes 196612
  355.7 4.8 copy-start.35
  355.7 4.8 copy-start.179
  382.2 6.6 %copy-start.141 = (f32[256,128]{1,0:T(8,128)S(1)}, f32[256,128]{1,0:T(8,128)}, u32[]{:S(2)}) copy-start(f32[256,128]{1,0:T(8,128)} %get-tuple-element.526) | copy-start | bytes 393220
  382.2 6.7 %copy-start.140 = (f32[256,128]{1,0:T(8,128)S(1)}, f32[256,128]{1,0:T(8,128)}, u32[]{:S(2)}) copy-start(f32[256,128]{1,0:T(8,128)} %get-tuple-element.522) | copy-start | bytes 393220
  382.2 7.7 %copy-start.139 = (f32[256,128]{1,0:T(8,128)S(1)}, f32[256,128]{1,0:T(8,128)}, u32[]{:S(2)}) copy-start(f32[256,128]{1,0:T(8,128)} %get-tuple-element.514) | copy-start | bytes 393220
  382.2 7.8 %copy-start.138 = (f32[256,128]{1,0:T(8,128)S(1)}, f32[256,128]{1,0:T(8,128)}, u32[]{:S(2)}) copy-start(f32[256,128]{1,0:T(8,128)} %get-tuple-element.510) | copy-start | bytes 393220
  382.2 9.7 %copy-start.137 = (f32[256,128]{1,0:T(8,128)S(1)}, f32[256,128]{1,0:T(8,128)}, u32[]{:S(2)}) copy-start(f32[256,128]{1,0:T(8,128)} %get-tuple-element.498) | copy-start | bytes 393220
  382.2 9.7 %copy-start.136 = (f32[256,128]{1,0:T(8,128)S(1)}, f32[256,128]{1,0:T(8,128)}, u32[]{:S(2)}) copy-start(f32[256,128]{1,0:T(8,128)} %get-tuple-element.494) | copy-start | bytes 393220
  382.2 9.8 %copy-start.135 = (f32[256,128]{1,0:T(8,128)S(1)}, f32[256,128]{1,0:T(8,128)}, u32[]{:S(2)}) copy-start(f32[256,128]{1,0:T(8,128)} %get-tuple-element.490) | copy-start | bytes 393220
  382.3 10.8 %copy-start.134 = (f32[256,128]{1,0:T(8,128)S(1)}, f32[256,128]{1,0:T(8,128)}, u32[]{:S(2)}) copy-start(f32[256,128]{1,0:T(8,128)} %get-tuple-element.482) | copy-start | bytes 393220
  382.3 10.8 %copy-start.133 = (f32[256,128]{1,0:T(8,128)S(1)}, f32[256,128]{1,0:T(8,128)}, u32[]{:S(2)}) copy-start(f32[256,128]{1,0:T(8,128)} %get-tuple-element.478) | copy-start | bytes 393220
  382.3 56.7 %all-to-all-start.5 = ((f32[32,128,128]{2,1,0:T(8,128)}), f32[32,128,128]{2,1,0:T(8,128)}, u32[]{:S(2)}, u32[]{:S(2)}) async-start(f32[32,128,128]{2,1,0:T(8,128)} %bitcast.234), calls=%async_computation.5 | async-start | bytes 4194304 | tf_op jit(solution)/shard_map/all_to_all | solution.py:108
  388.8 5.3 copy-start.149
  388.8 5.3 copy-start.132
  (164 other events, 424.5 us)
where the time goes:
time: 555 us; the launch traced here: 549 us
  blocking collectives  140 us (25%)
  waiting for transfers between devices  124 us (22%)
  matrix products  124 us (22%)
  local copies, waits for them, and re-layouts  80.8 us (15%)
  starting transfers between devices  46.9 us (8%)
  other arithmetic  30.6 us (6%)
    psum x1, blocking collectives, local(): keyvalue_bias_gradient = lax.psum(local_sums, ('dp', 'seq')) * root_norm  104 us
    dot_general x16, matrix products, block_grads(): jnp.einsum('hbk,bhd->kd', probs_half, gradient_rows, preferred_element_ty...  38.6 us
    psum x1, blocking collectives, local(): lax.psum(query_sum, 'dp').reshape(per_dev, HEAD_SIZE) * root_norm  35.7 us
    dot_general x16, matrix products, block_grads(): jnp.einsum('hbk,bhd->kd', dscores, query_row_block, preferred_element_typ...  34.2 us
    all_to_all x1, waiting for transfers between devices, local(): lax.all_to_all(spread_heads(key_input, replica_count), 'seq', split_axis=...  28.1 us
    unnamed x446, local copies, waits for them, and re-layouts  27.4 us
    all_to_all x1, waiting for transfers between devices, local(): lax.all_to_all(spread_heads(value_input, replica_count), 'seq', split_axi...  25.1 us
    convert_element_type x16, local copies, waits for them, and re-layouts, block_grads(): delta = jnp.sum(gradient_rows.astype(jnp.float32) * output, axis=2)  24.9 us
  transfers between devices with their start and end apart: 7, of which 7 were waited for; matrix products, arithmetic and copies ran while one was open for 15% of the time, Pallas kernels for 0%

commit v1 on v0

v1 whole, which is shorter than its diff:
```python
import functools
import math

import jax
import jax.numpy as jnp
from jax import lax
from jax.experimental import pallas as pl
from jax.experimental.pallas import tpu as pltpu
from jax.sharding import PartitionSpec as P

QUERY_HEADS = 32
KEYVALUE_HEADS = 4
HEAD_SIZE = 128
GROUP = QUERY_HEADS // KEYVALUE_HEADS
ROWS = 128
BLOCK = 256
CHUNKS = 8
SPAN = BLOCK * CHUNKS
HALF = 16
SLOTS = 3
FAR = 6
COLS = GROUP * HEAD_SIZE
SCALE = 1.0 / math.sqrt(HEAD_SIZE)
SCALE2 = SCALE * math.log2(math.e)

F32 = jnp.float32
BF16 = jnp.bfloat16
MESH = pl.DeviceIdType.MESH
NT = (((1,), (1,)), ((), ()))
NN = (((1,), (0,)), ((), ()))
TN = (((0,), (0,)), ((), ()))


def dot(a, b, dims):
    return lax.dot_general(a, b, dims, preferred_element_type=F32)


def fold(x, op):
    return op(x.reshape(x.shape[0] // 8, 8, x.shape[1]), axis=0)


def at(start, size):
    return pl.ds(pl.multiple_of(start, size), size)


def host(half, chunk, side, core):
    far = chunk // FAR if side else 0
    device = ((half + far) % 2) * HALF + (chunk - FAR * far) * 2 + core
    return device, side + far


def send(src, dst, send_sem, recv_sem, device, me):
    @pl.when(device != me)
    def _():
        pltpu.make_async_remote_copy(
            src, dst, send_sem, recv_sem, device_id={"seq": device}, device_id_type=MESH
        ).start()

    @pl.when(device == me)
    def _():
        pltpu.make_async_copy(src, dst, recv_sem).start()


def sent(src, dst, send_sem, recv_sem, device, me):
    @pl.when(device != me)
    def _():
        pltpu.make_async_remote_copy(
            src, dst, send_sem, recv_sem, device_id={"seq": device}, device_id_type=MESH
        ).wait_send()


def landed(ref, sem):
    pltpu.make_async_copy(ref, ref, sem).wait()


def main_kernel(
    q_in, k_in, v_in, g_in,
    dq_out, dk_out, dv_out, qb_out, kvb_out,
    qs, gs, ks, vs, scores, dprobs, dqs, dkst, dvst, dqst, rk, rv, qb, kvb, rqb, rkvb,
    q_send, q_recv, k_send, k_recv, d_send, d_recv, dq_send, dq_recv, b_send, b_recv, kvb_send, kvb_recv,
):
    me = lax.axis_index("seq")
    half = me // HALF
    index = me % HALF
    chunk = index // 2
    core = index % 2

    barrier = pltpu.get_barrier_semaphore()

    def greet(step, carry):
        other = (me + step) % (2 * HALF)
        pl.semaphore_signal(barrier, inc=1, device_id={"seq": other}, device_id_type=MESH)
        return carry

    lax.fori_loop(1, 2 * HALF, greet, 0)
    pl.semaphore_wait(barrier, 2 * HALF - 1)

    def spread(act):
        for side in range(2):
            for part in range(2):
                rows_in, rows_at = ((q_in, qs), (g_in, gs))[part]
                keys_in, keys_at = ((k_in, ks), (v_in, vs))[part]
                for to in range(2):
                    head = 2 * to + side
                    device, slot = host(half, chunk, side, to)
                    act(
                        rows_in.at[:, pl.ds(head * COLS, COLS)],
                        rows_at.at[slot, at(core * ROWS, ROWS)],
                        q_send.at[head, part],
                        q_recv.at[slot, part],
                        device,
                        me,
                    )

                def step(i, carry):
                    later = CHUNKS - 1 - i
                    for to in range(2):
                        head = 2 * to + side
                        device, slot = host(half, later, side, to)
                        act(
                            keys_in.at[:, pl.ds(head * HEAD_SIZE, HEAD_SIZE)],
                            keys_at.at[slot, at(index * ROWS, ROWS)],
                            k_send.at[later, head, part],
                            k_recv.at[slot, chunk, part],
                            device,
                            me,
                        )
                    return carry

                lax.fori_loop(0, CHUNKS - chunk, step, 0)

    spread(send)

    key_ids = lax.broadcasted_iota(jnp.int32, (BLOCK, BLOCK), 0)
    query_ids = lax.broadcasted_iota(jnp.int32, (BLOCK, BLOCK), 1)
    cols = [pl.ds(j * HEAD_SIZE, HEAD_SIZE) for j in range(GROUP)]

    def where_job(slot):
        far = slot // 2
        return (half + far) % 2, chunk + FAR * far, 2 * core + (slot + 1) // 2

    def back(act, slot, block):
        job_half, job_chunk, head = where_job(slot)
        for part in range(2):
            stage, place = ((dkst, rk), (dvst, rv))[part]
            for to in range(2):
                act(
                    stage.at[slot, at(block * BLOCK + to * ROWS, ROWS)],
                    place.at[job_chunk, :, at(head * HEAD_SIZE, HEAD_SIZE)],
                    d_send.at[slot, block, to, part],
                    d_recv.at[job_chunk, part],
                    job_half * HALF + block * 2 + to,
                    me,
                )

    def back_rows(act, slot):
        job_half, job_chunk, head = where_job(slot)
        for to in range(2):
            act(
                dqst.at[slot, pl.ds(to * ROWS, ROWS)],
                dq_out.at[:, at(head * COLS, COLS)],
                dq_send.at[slot, to],
                dq_recv,
                job_half * HALF + job_chunk * 2 + to,
                me,
            )

    def back_bias(act, slot):
        job_half, job_chunk, head = where_job(slot)
        source = job_half * CHUNKS + job_chunk
        act(kvb.at[slot], rkvb.at[source], kvb_send.at[slot], kvb_recv, head * GROUP, me)
        for j in range(GROUP):
            act(
                qb.at[slot * GROUP + j],
                rqb.at[source],
                b_send.at[slot, j],
                b_recv,
                head * GROUP + j,
                me,
            )

    def job(slot, carry):
        _, job_chunk, _ = where_job(slot)

        def pass_scores(block, peaks, diagonal):
            landed(ks.at[slot, at(block * BLOCK, BLOCK)], k_recv.at[slot, block, 0])
            rows = at(block * BLOCK, BLOCK)
            key_block = ks[slot, rows, :]
            out = []
            for j in range(GROUP):
                s = dot(key_block, qs[slot, :, cols[j]], NT)
                if diagonal:
                    s = jnp.where(key_ids <= query_ids, s, -jnp.inf)
                scores[j, rows, :] = s
                out.append(jnp.maximum(peaks[j], fold(s, jnp.max)))
            return tuple(out)

        landed(qs.at[slot], q_recv.at[slot, 0])
        peaks = tuple(jnp.full((8, BLOCK), -jnp.inf, F32) for _ in range(GROUP))
        peaks = pass_scores(job_chunk, peaks, True)
        peaks = lax.fori_loop(
            0, job_chunk, lambda i, c: pass_scores(job_chunk - 1 - i, c, False), peaks
        )
        peaks = [jnp.max(x, axis=0, keepdims=True) * SCALE2 for x in peaks]

        def pass_probs(i, sums):
            block = job_chunk - i
            landed(vs.at[slot, at(block * BLOCK, BLOCK)], k_recv.at[slot, block, 1])
            rows = at(block * BLOCK, BLOCK)
            value_block = vs[slot, rows, :]
            out = []
            for j in range(GROUP):
                p = jnp.exp2(scores[j, rows, :] * SCALE2 - peaks[j])
                dp = dot(value_block, gs[slot, :, cols[j]], NT)
                scores[j, rows, :] = p
                dprobs[j, rows, :] = dp
                out.append((sums[j][0] + fold(p, jnp.sum), sums[j][1] + fold(p * dp, jnp.sum)))
            return tuple(out)

        landed(gs.at[slot], q_recv.at[slot, 1])
        zero = jnp.zeros((8, BLOCK), F32)
        sums = lax.fori_loop(
            0, job_chunk + 1, pass_probs, tuple((zero, zero) for _ in range(GROUP))
        )
        inverse = [1.0 / jnp.sum(x[0], axis=0, keepdims=True) for x in sums]
        delta = [jnp.sum(x[1], axis=0, keepdims=True) * r for x, r in zip(sums, inverse)]

        dqs[...] = jnp.zeros_like(dqs)

        def pass_grads(i, bias):
            block = job_chunk - i
            rows = at(block * BLOCK, BLOCK)
            key_block = ks[slot, rows, :]
            dv = jnp.zeros((BLOCK, HEAD_SIZE), F32)
            dk = jnp.zeros((BLOCK, HEAD_SIZE), F32)
            for j in range(GROUP):
                p = scores[j, rows, :] * inverse[j]
                ds = (p * (dprobs[j, rows, :] - delta[j])).astype(BF16)
                dv = dv + dot(p.astype(BF16), gs[slot, :, cols[j]], NN)
                dk = dk + dot(ds, qs[slot, :, cols[j]], NN)
                dqs[:, cols[j]] += dot(ds, key_block, TN)
            dk = dk * SCALE
            dkst[slot, rows, :] = dk.astype(BF16)
            dvst[slot, rows, :] = dv.astype(BF16)
            back(send, slot, block)
            return bias[0] + fold(dk, jnp.sum), bias[1] + fold(dv, jnp.sum)

        zero = jnp.zeros((8, HEAD_SIZE), F32)
        bias = lax.fori_loop(0, job_chunk + 1, pass_grads, (zero, zero))
        for part in range(2):
            kvb[slot, pl.ds(part, 1), :] = jnp.sum(bias[part], axis=0, keepdims=True)
        for j in range(GROUP):
            x = dqs[:, cols[j]] * SCALE
            dqst[slot, :, cols[j]] = x.astype(BF16)
            qb[slot * GROUP + j] = jnp.sum(fold(x, jnp.sum), axis=0, keepdims=True)
        back_bias(send, slot)
        back_rows(send, slot)
        return carry

    jobs = SLOTS - (chunk + 2) // 4
    lax.fori_loop(0, jobs, job, 0)

    landed(rqb, b_recv)
    qb_out[...] = jnp.sum(rqb[...], axis=0)

    @pl.when(me % GROUP == 0)
    def _():
        landed(rkvb, kvb_recv)
        kvb_out[...] = jnp.sum(rkvb[...], axis=0)

    @pl.when(me % GROUP != 0)
    def _():
        kvb_out[...] = jnp.zeros_like(kvb_out)

    for part in range(2):
        place, out = ((rk, dk_out), (rv, dv_out))[part]

        def gather(later, total):
            landed(place.at[later], d_recv.at[later, part])
            return total + place[later].astype(F32)

        total = jnp.zeros((ROWS, KEYVALUE_HEADS * HEAD_SIZE), F32)
        out[...] = lax.fori_loop(chunk, CHUNKS, gather, total).astype(BF16)

    landed(dq_out, dq_recv)

    spread(sent)

    def close(slot, carry):
        _, job_chunk, _ = where_job(slot)

        def step(block, c):
            back(sent, slot, block)
            return c

        lax.fori_loop(0, job_chunk + 1, step, 0)
        back_bias(sent, slot)
        back_rows(sent, slot)
        return carry

    lax.fori_loop(0, jobs, close, 0)


def bias_kernel(groups, norm, qb_in, kvb_in, qb_out, kvb_out, mine, theirs, kv, all_kv,
                x_send, x_recv, y_send, y_recv):
    me = lax.axis_index("seq")
    group = lax.axis_index("dp")
    members = 2 * HALF
    barrier = pltpu.get_barrier_semaphore()

    def greet_group(step, carry):
        other = (group + step) % groups
        pl.semaphore_signal(barrier, inc=1, device_id={"dp": other}, device_id_type=MESH)
        return carry

    def greet(step, carry):
        other = (me + step) % members
        pl.semaphore_signal(barrier, inc=1, device_id={"seq": other}, device_id_type=MESH)
        return carry

    lax.fori_loop(1, groups, greet_group, 0)
    lax.fori_loop(1, members, greet, 0)
    mine[pl.ds(0, 1), :] = qb_in[...]
    mine[pl.ds(1, 2), :] = kvb_in[...]
    mine[pl.ds(3, 5), :] = jnp.zeros((5, HEAD_SIZE), F32)
    pl.semaphore_wait(barrier, groups - 1 + members - 1)

    def across(step):
        return pltpu.make_async_remote_copy(
            mine, theirs.at[step - 1], x_send.at[step - 1], x_recv,
            device_id={"dp": (group + step) % groups}, device_id_type=MESH,
        )

    def start(step, carry):
        across(step).start()
        return carry

    lax.fori_loop(1, groups, start, 0)
    landed(theirs, x_recv)
    total = (mine[...] + jnp.sum(theirs[...], axis=0)) * norm
    qb_out[...] = total[0:1]
    kv[...] = total[1:3]

    def along(step):
        return pltpu.make_async_remote_copy(
            kv, all_kv.at[me // GROUP], y_send.at[step - 1], y_recv,
            device_id={"seq": (me + step) % members}, device_id_type=MESH,
        )

    @pl.when(me % GROUP == 0)
    def _():
        def start(step, carry):
            along(step).start()
            return carry

        lax.fori_loop(1, members, start, 0)
        pltpu.make_async_copy(kv, all_kv.at[me // GROUP], y_recv).start()

    landed(all_kv, y_recv)
    for head in range(KEYVALUE_HEADS):
        kvb_out[:, pl.ds(head * HEAD_SIZE, HEAD_SIZE)] = all_kv[head]

    def finish(step, carry):
        across(step).wait_send()
        return carry

    lax.fori_loop(1, groups, finish, 0)

    @pl.when(me % GROUP == 0)
    def _():
        def finish(step, carry):
            along(step).wait_send()
            return carry

        lax.fori_loop(1, members, finish, 0)


def local(query_input, key_input, value_input, output_gradient):
    groups = lax.axis_size("dp")
    vmem = pl.BlockSpec(memory_space=pltpu.VMEM)
    any_space = pl.BlockSpec(memory_space=pl.ANY)
    dma = pltpu.SemaphoreType.DMA
    kv_cols = KEYVALUE_HEADS * HEAD_SIZE
    grad_query, grad_key, grad_value, query_sum, keyvalue_sum = pl.pallas_call(
        main_kernel,
        out_shape=[
            jax.ShapeDtypeStruct((ROWS, QUERY_HEADS * HEAD_SIZE), BF16),
            jax.ShapeDtypeStruct((ROWS, kv_cols), BF16),
            jax.ShapeDtypeStruct((ROWS, kv_cols), BF16),
            jax.ShapeDtypeStruct((1, HEAD_SIZE), F32),
            jax.ShapeDtypeStruct((2, HEAD_SIZE), F32),
        ],
        in_specs=[any_space] * 4,
        out_specs=[any_space, vmem, vmem, vmem, vmem],
        scratch_shapes=[
            pltpu.VMEM((SLOTS, BLOCK, COLS), BF16),
            pltpu.VMEM((SLOTS, BLOCK, COLS), BF16),
            pltpu.VMEM((SLOTS, SPAN, HEAD_SIZE), BF16),
            pltpu.VMEM((SLOTS, SPAN, HEAD_SIZE), BF16),
            pltpu.VMEM((GROUP, SPAN, BLOCK), F32),
            pltpu.VMEM((GROUP, SPAN, BLOCK), F32),
            pltpu.VMEM((BLOCK, COLS), F32),
            pltpu.VMEM((SLOTS, SPAN, HEAD_SIZE), BF16),
            pltpu.VMEM((SLOTS, SPAN, HEAD_SIZE), BF16),
            pltpu.VMEM((SLOTS, BLOCK, COLS), BF16),
            pltpu.VMEM((CHUNKS, ROWS, kv_cols), BF16),
            pltpu.VMEM((CHUNKS, ROWS, kv_cols), BF16),
            pltpu.VMEM((SLOTS * GROUP, 1, HEAD_SIZE), F32),
            pltpu.VMEM((SLOTS, 2, HEAD_SIZE), F32),
            pltpu.VMEM((2 * CHUNKS, 1, HEAD_SIZE), F32),
            pltpu.VMEM((2 * CHUNKS, 2, HEAD_SIZE), F32),
            dma((KEYVALUE_HEADS, 2)),
            dma((SLOTS, 2)),
            dma((CHUNKS, KEYVALUE_HEADS, 2)),
            dma((SLOTS, CHUNKS, 2)),
            dma((SLOTS, CHUNKS, 2, 2)),
            dma((CHUNKS, 2)),
            dma((SLOTS, 2)),
            dma,
            dma((SLOTS, GROUP)),
            dma,
            dma((SLOTS,)),
            dma,
        ],
        compiler_params=pltpu.CompilerParams(
            collective_id=0, has_side_effects=True, vmem_limit_bytes=60 * 2**20
        ),
        name="attention_grads",
    )(query_input, key_input, value_input, output_gradient)
    norm = 1.0 / math.sqrt(ROWS * 2 * HALF * groups)
    query_bias, keyvalue_bias = pl.pallas_call(
        functools.partial(bias_kernel, groups, norm),
        out_shape=[
            jax.ShapeDtypeStruct((1, HEAD_SIZE), F32),
            jax.ShapeDtypeStruct((2, kv_cols), F32),
        ],
        in_specs=[vmem] * 2,
        out_specs=[vmem] * 2,
        scratch_shapes=[
            pltpu.VMEM((8, HEAD_SIZE), F32),
            pltpu.VMEM((groups - 1, 8, HEAD_SIZE), F32),
            pltpu.VMEM((2, HEAD_SIZE), F32),
            pltpu.VMEM((KEYVALUE_HEADS, 2, HEAD_SIZE), F32),
            dma((groups - 1,)),
            dma,
            dma((2 * HALF - 1,)),
            dma,
        ],
        compiler_params=pltpu.CompilerParams(collective_id=1, has_side_effects=True),
        name="bias_sums",
    )(query_sum, keyvalue_sum)
    return grad_query, grad_key, grad_value, query_bias, keyvalue_bias


def solution(mesh):
    rows = P(("dp", "seq"), None)
    return jax.shard_map(
        local,
        mesh=mesh,
        in_specs=(rows,) * 4,
        out_specs=(rows, rows, rows, P("seq", None), P()),
        check_vma=False,
    )
```

time: 555 us -> 125 us (0.23); the launches traced: 549 us -> 125 us
  blocking collectives: 140 us -> 0 us
  matrix products: 124 us -> 0 us
  waiting for transfers between devices: 124 us -> 0 us
  Pallas kernels: 0 us -> 119 us
  local copies, waits for them, and re-layouts: 80.8 us -> 5.05 us
  starting transfers between devices: 46.9 us -> 0 us
  other arithmetic: 30.6 us -> 0 us
    psum x2 -> x0, blocking collectives: 140 us -> none  [the longest x1 104 us: local(): keyvalue_bias_gradient = lax.psum(local_sums, ('dp', 'seq')) * root_norm]
    dot_general x96 -> x0, matrix products: 124 us -> none  [the longest x16 38.6 us: block_grads(): jnp.einsum('hbk,bhd->kd', probs_half, gradient_rows, preferred_element_ty...]
    all_to_all x7 -> x0, waiting for transfers between devices: 124 us -> none  [the longest x1 28.1 us: local(): lax.all_to_all(spread_heads(key_input, replica_count), 'seq', split_axis=...]
    pallas_call x0 -> x2, Pallas kernels: none -> 119 us  [the longest x1 96.6 us: local(): pl.pallas_call(main_kernel, out_shape=[jax.ShapeDtypeStruct((ROWS, QUERY_...]
    all_to_all x7 -> x0, starting transfers between devices: 46.9 us -> none  [the longest x1 11.2 us: local(): lax.all_to_all(spread_heads(key_input, replica_count), 'seq', split_axis=...]
    convert_element_type x18 -> x0, local copies, waits for them, and re-layouts: 25.1 us -> none  [the longest x16 24.9 us: block_grads(): delta = jnp.sum(gradient_rows.astype(jnp.float32) * output, axis=2)]
    unnamed x446 -> x13, local copies, waits for them, and re-layouts: 27.4 us -> 5.05 us
    slice x34 -> x0, local copies, waits for them, and re-layouts: 19.5 us -> none  [the longest x8 6.91 us: local(): value_row_block = head_value[seq_start:row_end]]
  transfers between devices with their start and end apart: 7 -> 0, of which waited for: 7 -> 0; matrix products, arithmetic and copies ran while one was open for 15% -> 0% of each run, Pallas kernels for 0% -> 0%
where the time goes in v1:
time: 125 us
  Pallas kernels  119 us (95%)
  local copies, waits for them, and re-layouts  5.05 us (4%)
    pallas_call x1, Pallas kernels, local(): pl.pallas_call(main_kernel, out_shape=[jax.ShapeDtypeStruct((ROWS, QUERY_...  96.6 us
    pallas_call x1, Pallas kernels, local(): pl.pallas_call(functools.partial(bias_kernel, groups, norm), out_shape=[j...  22.9 us
    unnamed x13, local copies, waits for them, and re-layouts  5.05 us

profile of v1, /device:TPU:1, one launch (start us, length us, event | category | flops | bytes accessed | tf_op | source)
XLA Modules:
  0.0 125.2 jit_solution(6780813339845589263)
XLA Ops:
  0.6 96.6 %attention_grads.1 = (bf16[128,4096]{1,0:T(8,128)(2,1)}, bf16[128,512]{1,0:T(8,128)(2,1)}, bf16[128,512]{1,0:T(8,128)(2,1)}, f32[1,128]{1,0:T(1,128)}, f32[2,128]{1,0:T(2,128)}) custom-call(bf16[128,4096]{1,0:T(8,128)(2,1)} %q_in.1, bf16[128,512]{1,0:T(8,128)(2,1)} %k_in.1, bf16[128,512]{1,0:T(8,128)(2,1)} %v_in.1, bf16[128,4096]{1,0:T(8,128)(2,1)} %g_in.1), custom_call_target="tpu_custom_call" | custom-call | tf_op jit(solution)/shard_map/attention_grads/pallas_call | solution.py:384
  97.2 22.9 %bias_sums.1 = (f32[1,128]{1,0:T(1,128)}, f32[2,512]{1,0:T(2,128)}) custom-call(f32[1,128]{1,0:T(1,128)} %get-tuple-element.15.qb_in, f32[2,128]{1,0:T(2,128)} %get-tuple-element.16.kvb_in), custom_call_target="tpu_custom_call" | custom-call | tf_op jit(solution)/shard_map/bias_sums/pallas_call | solution.py:431
  120.1 0.0 copy-start.1
  120.1 2.3 %copy.14 = bf16[128,4096]{1,0:T(8,128)(2,1)} copy(bf16[128,4096]{1,0:T(8,128)(2,1)} %get-tuple-element.24) | data formatting | bytes 2097152
  122.5 0.0 copy-done.1
  122.5 0.0 copy-start
  122.5 0.7 copy.15
  123.1 0.3 copy-done
  123.4 0.0 copy-start.3
  123.4 0.0 copy-start.2
  123.4 0.7 copy.16
  124.1 0.0 copy-done.3
  124.1 0.5 copy.17
  124.6 0.0 copy-done.2
  124.6 0.6 copy.18
Async XLA Ops:
  120.1 2.3 %copy-start.1 = (bf16[128,512]{1,0:T(8,128)(2,1)S(1)}, bf16[128,512]{1,0:T(8,128)(2,1)}, u32[]{:S(2)}) copy-start(bf16[128,512]{1,0:T(8,128)(2,1)} %get-tuple-element.25) | copy-start | bytes 393220
  122.5 1.0 copy-start
  123.4 0.7 copy-start.3
  123.4 1.2 copy-start.2

commit v2 on v1

v2 whole, which is shorter than its diff:
```python
import functools
import math

import jax
import jax.numpy as jnp
from jax import lax
from jax.experimental import pallas as pl
from jax.experimental.pallas import tpu as pltpu
from jax.sharding import PartitionSpec as P

QUERY_HEADS = 32
KEYVALUE_HEADS = 4
HEAD_SIZE = 128
GROUP = QUERY_HEADS // KEYVALUE_HEADS
ROWS = 128
BLOCK = 256
CHUNKS = 8
SPAN = BLOCK * CHUNKS
HALF = 16
SLOTS = 2
LINE = 4
COLS = GROUP * HEAD_SIZE
SCALE = 1.0 / math.sqrt(HEAD_SIZE)
SCALE2 = SCALE * math.log2(math.e)

F32 = jnp.float32
BF16 = jnp.bfloat16
MESH = pl.DeviceIdType.MESH
NT = (((1,), (1,)), ((), ()))
NN = (((1,), (0,)), ((), ()))
TN = (((0,), (0,)), ((), ()))


def dot(a, b, dims):
    return lax.dot_general(a, b, dims, preferred_element_type=F32)


def fold(x, op):
    return op(x.reshape(x.shape[0] // 8, 8, x.shape[1]), axis=0)


def at(start, size):
    return pl.ds(pl.multiple_of(start, size), size)


def remote(src, dst, send_sem, recv_sem, device):
    return pltpu.make_async_remote_copy(
        src, dst, send_sem, recv_sem, device_id=device, device_id_type=MESH
    )


def send(src, dst, send_sem, recv_sem, device, me):
    @pl.when(device != me)
    def _():
        remote(src, dst, send_sem, recv_sem, {"seq": device}).start()

    @pl.when(device == me)
    def _():
        pltpu.make_async_copy(src, dst, recv_sem).start()


def sent(src, dst, send_sem, recv_sem, device, me):
    @pl.when(device != me)
    def _():
        remote(src, dst, send_sem, recv_sem, {"seq": device}).wait_send()


def landed(ref, sem):
    pltpu.make_async_copy(ref, ref, sem).wait()


def each(start, stop, act):
    def step(i, carry):
        act(i)
        return carry

    lax.fori_loop(start, stop, step, 0)


def kernel(
    groups, norm,
    q_in, k_in, v_in, g_in,
    dq_out, dk_out, dv_out, qb_out, kvb_out,
    qs, gs, ks, vs, scores, dprobs, dqs, dkst, dvst, dqst, rk, rv, met,
    notes, notes_in, over_groups, groups_in, over_halves, halves_in,
    q_send, q_recv, k_send, k_recv, x_send, d_send, d_recv, m_send, m_recv, dq_send, dq_recv,
    n_send, n_recv, g_send, g_recv, h_send, h_recv,
):
    me = lax.axis_index("seq")
    group = lax.axis_index("dp")
    base = me // HALF * HALF
    index = me % HALF
    chunk = index // 2
    core = index % 2
    row = index // LINE
    column = chunk % 2
    beside = me + 2 - 4 * column
    opposite = (me + HALF) % (2 * HALF)

    barrier = pltpu.get_barrier_semaphore()

    def greet(device):
        pl.semaphore_signal(barrier, inc=1, device_id=device, device_id_type=MESH)

    each(1, HALF, lambda i: greet({"seq": base + (index + i) % HALF}))
    each(1, groups, lambda i: greet({"dp": (group + i) % groups}))
    greet({"seq": opposite})
    pl.semaphore_wait(barrier, HALF - 1 + groups - 1 + 1)

    def spread(act):
        for slot in range(SLOTS):
            for part in range(2):
                rows_in, rows_at = ((q_in, qs), (g_in, gs))[part]
                keys_in, keys_at = ((k_in, ks), (v_in, vs))[part]
                for to in range(2):
                    head = 2 * to + slot
                    act(
                        rows_in.at[:, pl.ds(head * COLS, COLS)],
                        rows_at.at[slot, at(core * ROWS, ROWS)],
                        q_send.at[head, part],
                        q_recv.at[slot, part],
                        base + chunk * 2 + to,
                        me,
                    )

                def push(line, there, lane):
                    for to in range(2):
                        head = 2 * to + slot
                        act(
                            keys_in.at[:, pl.ds(head * HEAD_SIZE, HEAD_SIZE)],
                            keys_at.at[slot, at(index * ROWS, ROWS)],
                            k_send.at[lane, head, part],
                            k_recv.at[slot, chunk, part],
                            base + (line * 2 + there) * 2 + to,
                            me,
                        )

                each(0, LINE - row, lambda i: push(LINE - 1 - i, column, LINE - 1 - i))

                @pl.when(column == 0)
                def _():
                    push(row, 1, LINE)

    def across(slot, part, line, act):
        place = (ks, vs)[part]
        block = place.at[slot, at((2 * line + column) * BLOCK, BLOCK)]
        sem = k_recv.at[slot, 2 * line + column, part]
        act(block, sem, x_send.at[slot, part, line])

    def hand_on(block, sem, out_sem):
        landed(block, sem)
        remote(block, block, out_sem, sem, {"seq": beside}).start()

    def handed_on(block, sem, out_sem):
        remote(block, block, out_sem, sem, {"seq": beside}).wait_send()

    spread(send)
    each(0, row, lambda i: across(0, 0, row - 1 - i, hand_on))

    first = 2 * row
    key_ids = lax.broadcasted_iota(jnp.int32, (BLOCK, BLOCK), 0)
    query_ids = lax.broadcasted_iota(jnp.int32, (BLOCK, BLOCK), 1)
    cols = [pl.ds(j * HEAD_SIZE, HEAD_SIZE) for j in range(GROUP)]

    def back(act, slot, block, place_at):
        head = 2 * core + slot
        for part in range(2):
            stage, place = ((dkst, rk), (dvst, rv))[part]
            for to in range(2):
                act(
                    stage.at[slot, at(block * BLOCK + to * ROWS, ROWS)],
                    place.at[place_at, :, at(head * HEAD_SIZE, HEAD_SIZE)],
                    d_send.at[slot, block, to, part],
                    d_recv.at[place_at, part],
                    base + block * 2 + to,
                    me,
                )

    def back_own(act, slot):
        back(act, slot, chunk, row)

        @pl.when(column == 1)
        def _():
            back(act, slot, first, LINE)

    def back_across(act, slot, line):
        block = 2 * line + 1 - column
        for part in range(2):
            act(
                (dkst, dvst)[part].at[slot, at(block * BLOCK, BLOCK)],
                met.at[slot, part, line],
                m_send.at[slot, part, line],
                m_recv.at[slot, part, line],
                beside,
                me,
            )

    def settle(slot, line):
        rows = at((2 * line + column) * BLOCK, BLOCK)
        for part in range(2):
            stage = (dkst, dvst)[part]
            landed(met.at[slot, part, line], m_recv.at[slot, part, line])
            total = stage[slot, rows, :].astype(F32) + met[slot, part, line].astype(F32)
            stage[slot, rows, :] = total.astype(BF16)
        back(send, slot, 2 * line + column, row)

    def back_rows(act, slot):
        head = 2 * core + slot
        for to in range(2):
            act(
                dqst.at[slot, pl.ds(to * ROWS, ROWS)],
                dq_out.at[:, at(head * COLS, COLS)],
                dq_send.at[slot, to],
                dq_recv,
                base + chunk * 2 + to,
                me,
            )

    def job(slot, carry):
        def wait_block(block, part):
            place = (ks, vs)[part]
            landed(place.at[slot, at(block * BLOCK, BLOCK)], k_recv.at[slot, block, part])

        def walk(step, part, carry, next_slot, next_part):
            wait_block(chunk, part)
            carry = step(chunk, 1, carry, True)

            def partner(i, c):
                wait_block(first, part)
                return step(first, 1, c, False)

            carry = lax.fori_loop(0, column, partner, carry)

            def below(i, c):
                line = row - 1 - i
                wait_block(2 * line + 1 - column, part)
                c = step(2 * line, 2, c, False)

                @pl.when(slot == 0)
                def _():
                    across(next_slot, next_part, line, hand_on)

                return c

            return lax.fori_loop(0, row, below, carry)

        def pass_scores(block, size, peaks, diagonal):
            rows = pl.ds(pl.multiple_of(block * BLOCK, BLOCK), size * BLOCK)
            key_block = ks[slot, rows, :]
            out = []
            for j in range(GROUP):
                s = dot(key_block, qs[slot, :, cols[j]], NT)
                if diagonal:
                    s = jnp.where(key_ids <= query_ids, s, -jnp.inf)
                scores[j, rows, :] = s
                out.append(jnp.maximum(peaks[j], fold(s, jnp.max)))
            return tuple(out)

        landed(qs.at[slot], q_recv.at[slot, 0])
        peaks = tuple(jnp.full((8, BLOCK), -jnp.inf, F32) for _ in range(GROUP))
        peaks = walk(pass_scores, 0, peaks, 0, 1)
        peaks = [jnp.max(x, axis=0, keepdims=True) * SCALE2 for x in peaks]

        def pass_probs(block, size, sums, diagonal):
            rows = pl.ds(pl.multiple_of(block * BLOCK, BLOCK), size * BLOCK)
            value_block = vs[slot, rows, :]
            out = []
            for j in range(GROUP):
                p = jnp.exp2(scores[j, rows, :] * SCALE2 - peaks[j])
                dp = dot(value_block, gs[slot, :, cols[j]], NT)
                scores[j, rows, :] = p
                dprobs[j, rows, :] = dp
                out.append((sums[j][0] + fold(p, jnp.sum), sums[j][1] + fold(p * dp, jnp.sum)))
            return tuple(out)

        landed(gs.at[slot], q_recv.at[slot, 1])
        zero = jnp.zeros((8, BLOCK), F32)
        sums = tuple((zero, zero) for _ in range(GROUP))
        sums = walk(pass_probs, 1, sums, 1, 0)
        inverse = [1.0 / jnp.sum(x[0], axis=0, keepdims=True) for x in sums]
        delta = [jnp.sum(x[1], axis=0, keepdims=True) * r for x, r in zip(sums, inverse)]

        dqs[...] = jnp.zeros_like(dqs)

        def pass_grads(block, size, bias):
            rows = pl.ds(pl.multiple_of(block * BLOCK, BLOCK), size * BLOCK)
            key_columns = ks[slot, rows, :].T
            dv = jnp.zeros((size * BLOCK, HEAD_SIZE), F32)
            dk = jnp.zeros((size * BLOCK, HEAD_SIZE), F32)
            for j in range(GROUP):
                p = scores[j, rows, :] * inverse[j]
                ds = (p * (dprobs[j, rows, :] - delta[j])).astype(BF16)
                dv = dv + dot(p.astype(BF16), gs[slot, :, cols[j]], NN)
                dk = dk + dot(ds, qs[slot, :, cols[j]], NN)
                dqs[j] += dot(key_columns, ds, NN)
            dk = dk * SCALE
            dkst[slot, rows, :] = dk.astype(BF16)
            dvst[slot, rows, :] = dv.astype(BF16)
            return bias[0] + fold(dk, jnp.sum), bias[1] + fold(dv, jnp.sum)

        def grads_below(line, bias):
            bias = pass_grads(2 * line, 2, bias)

            back_across(send, slot, line)

            @pl.when(line > 0)
            def _():
                @pl.when(slot * (line - 1) == 0)
                def _():
                    settle(slot, line - 1)

            @pl.when(slot == 0)
            def _():
                across(1, 1, line, hand_on)

            return bias

        zero = jnp.zeros((8, HEAD_SIZE), F32)
        bias = lax.fori_loop(0, row, grads_below, (zero, zero))
        bias = lax.fori_loop(first, chunk + 1, lambda b, c: pass_grads(b, 1, c), bias)

        @pl.when(slot == 0)
        def _():
            back_own(send, slot)

            @pl.when(row > 0)
            def _():
                settle(slot, row - 1)

        for part in range(2):
            notes[0, pl.ds(1 + 2 * slot + part, 1), :] = jnp.sum(bias[part], axis=0, keepdims=True)
        for j in range(GROUP):
            x = dqs[j] * SCALE
            x = x.T
            dqst[slot, :, cols[j]] = x.astype(BF16)
            notes[slot * GROUP + j, pl.ds(0, 1), :] = jnp.sum(
                fold(x, jnp.sum), axis=0, keepdims=True
            )
        return carry

    notes[...] = jnp.zeros_like(notes)
    lax.fori_loop(0, SLOTS, job, 0)

    for i in range(1, HALF):
        notes[i, pl.ds(1, 4), :] = notes[0, pl.ds(1, 4), :]

    def tell(i, act):
        act(notes.at[i], notes_in.at[index], n_send.at[i], n_recv, base + i, me)

    each(0, HALF, lambda i: tell(i, send))
    back_own(send, 1)
    each(row // 2, row, lambda line: settle(1, line))
    for slot in range(SLOTS):
        back_rows(send, slot)

    landed(notes_in, n_recv)
    sums = [notes_in[0], notes_in[1]]
    for i in range(2, HALF):
        sums[i % 2] = sums[i % 2] + notes_in[i]
    for i in range(2):
        over_groups[i] = sums[i]

    def to_group(i):
        return remote(
            over_groups, groups_in.at[i - 1], g_send.at[i - 1], g_recv, {"dp": (group + i) % groups}
        )

    each(1, groups, lambda i: to_group(i).start())
    landed(groups_in, g_recv)
    over_halves[...] = over_groups[...] + jnp.sum(groups_in[...], axis=0)
    to_half = remote(over_halves, halves_in, h_send, h_recv, {"seq": opposite})
    to_half.start()
    to_half.wait_recv()
    sums = (over_halves[...] + halves_in[...]) * norm
    qb_out[...] = jnp.where(base == 0, sums[0, 0:1], sums[1, 0:1])
    for head in range(KEYVALUE_HEADS):
        for part in range(2):
            at_row = 1 + 2 * (head % 2) + part
            kvb_out[pl.ds(part, 1), pl.ds(head * HEAD_SIZE, HEAD_SIZE)] = sums[
                head // 2, at_row : at_row + 1
            ]

    for part in range(2):
        place, out = ((rk, dk_out), (rv, dv_out))[part]

        def gather(source, so_far):
            landed(place.at[source], d_recv.at[source, part])
            return so_far + place[source].astype(F32)

        total = jnp.zeros((ROWS, KEYVALUE_HEADS * HEAD_SIZE), F32)
        out[...] = lax.fori_loop(row, LINE + 1 - column, gather, total).astype(BF16)

    landed(dq_out, dq_recv)

    spread(sent)
    for slot in range(SLOTS):
        for part in range(2):
            each(0, row, lambda line: across(slot, part, line, handed_on))
        back_own(sent, slot)
        each(0, row, lambda line: back(sent, slot, 2 * line + column, row))
        each(0, row, lambda line: back_across(sent, slot, line))
        back_rows(sent, slot)
    each(0, HALF, lambda i: tell(i, sent))
    each(1, groups, lambda i: to_group(i).wait_send())
    to_half.wait_send()


def local(query_input, key_input, value_input, output_gradient):
    groups = lax.axis_size("dp")
    norm = 1.0 / math.sqrt(ROWS * 2 * HALF * groups)
    vmem = pl.BlockSpec(memory_space=pltpu.VMEM)
    any_space = pl.BlockSpec(memory_space=pl.ANY)
    dma = pltpu.SemaphoreType.DMA
    kv_cols = KEYVALUE_HEADS * HEAD_SIZE
    return tuple(
        pl.pallas_call(
            functools.partial(kernel, groups, norm),
            out_shape=[
                jax.ShapeDtypeStruct((ROWS, QUERY_HEADS * HEAD_SIZE), BF16),
                jax.ShapeDtypeStruct((ROWS, kv_cols), BF16),
                jax.ShapeDtypeStruct((ROWS, kv_cols), BF16),
                jax.ShapeDtypeStruct((1, HEAD_SIZE), F32),
                jax.ShapeDtypeStruct((2, kv_cols), F32),
            ],
            in_specs=[any_space] * 4,
            out_specs=[any_space, vmem, vmem, vmem, vmem],
            scratch_shapes=[
                pltpu.VMEM((SLOTS, BLOCK, COLS), BF16),
                pltpu.VMEM((SLOTS, BLOCK, COLS), BF16),
                pltpu.VMEM((SLOTS, SPAN, HEAD_SIZE), BF16),
                pltpu.VMEM((SLOTS, SPAN, HEAD_SIZE), BF16),
                pltpu.VMEM((GROUP, SPAN, BLOCK), F32),
                pltpu.VMEM((GROUP, SPAN, BLOCK), F32),
                pltpu.VMEM((GROUP, HEAD_SIZE, BLOCK), F32),
                pltpu.VMEM((SLOTS, SPAN, HEAD_SIZE), BF16),
                pltpu.VMEM((SLOTS, SPAN, HEAD_SIZE), BF16),
                pltpu.VMEM((SLOTS, BLOCK, COLS), BF16),
                pltpu.VMEM((LINE + 1, ROWS, kv_cols), BF16),
                pltpu.VMEM((LINE + 1, ROWS, kv_cols), BF16),
                pltpu.VMEM((SLOTS, 2, LINE - 1, BLOCK, HEAD_SIZE), BF16),
                pltpu.VMEM((HALF, 8, HEAD_SIZE), F32),
                pltpu.VMEM((HALF, 8, HEAD_SIZE), F32),
                pltpu.VMEM((2, 8, HEAD_SIZE), F32),
                pltpu.VMEM((groups - 1, 2, 8, HEAD_SIZE), F32),
                pltpu.VMEM((2, 8, HEAD_SIZE), F32),
                pltpu.VMEM((2, 8, HEAD_SIZE), F32),
                dma((KEYVALUE_HEADS, 2)),
                dma((SLOTS, 2)),
                dma((LINE + 1, KEYVALUE_HEADS, 2)),
                dma((SLOTS, CHUNKS, 2)),
                dma((SLOTS, 2, LINE)),
                dma((SLOTS, CHUNKS, 2, 2)),
                dma((LINE + 1, 2)),
                dma((SLOTS, 2, LINE - 1)),
                dma((SLOTS, 2, LINE - 1)),
                dma((SLOTS, 2)),
                dma,
                dma((HALF,)),
                dma,
                dma((groups - 1,)),
                dma,
                dma,
                dma,
            ],
            compiler_params=pltpu.CompilerParams(
                collective_id=0, has_side_effects=True, vmem_limit_bytes=60 * 2**20
            ),
            name="attention_grads",
        )(query_input, key_input, value_input, output_gradient)
    )


def solution(mesh):
    rows = P(("dp", "seq"), None)
    return jax.shard_map(
        local,
        mesh=mesh,
        in_specs=(rows,) * 4,
        out_specs=(rows, rows, rows, P("seq", None), P()),
        check_vma=False,
    )
```

time: 125 us -> 97 us (0.78)
  Pallas kernels: 119 us -> 91 us
    pallas_call x2 -> x1, Pallas kernels: 119 us -> 91 us  [local(): pl.pallas_call(functools.partial(kernel, groups, norm), out_shape=[jax.Sh...]
where the time goes in v2:
time: 97 us; the launch traced here: 96.7 us
  Pallas kernels  91 us (94%)
  local copies, waits for them, and re-layouts  5.04 us (5%)
    pallas_call x1, Pallas kernels, local(): pl.pallas_call(functools.partial(kernel, groups, norm), out_shape=[jax.Sh...  91 us
    unnamed x13, local copies, waits for them, and re-layouts  5.04 us

profile of v2, /device:TPU:1, one launch (start us, length us, event | category | flops | bytes accessed | tf_op | source)
XLA Modules:
  0.0 96.7 jit_solution(7512288246541070255)
XLA Ops:
  0.6 91.0 %attention_grads.1 = (bf16[128,4096]{1,0:T(8,128)(2,1)}, bf16[128,512]{1,0:T(8,128)(2,1)}, bf16[128,512]{1,0:T(8,128)(2,1)}, f32[1,128]{1,0:T(1,128)}, f32[2,512]{1,0:T(2,128)}) custom-call(bf16[128,4096]{1,0:T(8,128)(2,1)} %q_in.1, bf16[128,512]{1,0:T(8,128)(2,1)} %k_in.1, bf16[128,512]{1,0:T(8,128)(2,1)} %v_in.1, bf16[128,4096]{1,0:T(8,128)(2,1)} %g_in.1), custom_call_target="tpu_custom_call" | custom-call | tf_op jit(solution)/shard_map/attention_grads/pallas_call | solution.py:416
  91.7 0.0 copy-start.1
  91.7 2.3 %copy.14 = bf16[128,4096]{1,0:T(8,128)(2,1)} copy(bf16[128,4096]{1,0:T(8,128)(2,1)} %get-tuple-element.10) | data formatting | bytes 2097152
  94.0 0.0 copy-done.1
  94.0 0.0 copy-start
  94.0 0.7 copy.15
  94.7 0.3 copy-done
  94.9 0.0 copy-start.3
  95.0 0.0 copy-start.2
  95.0 0.7 copy.16
  95.6 0.0 copy-done.3
  95.6 0.5 copy.17
  96.1 0.0 copy-done.2
  96.1 0.6 copy.18
Async XLA Ops:
  91.7 2.3 %copy-start.1 = (bf16[128,512]{1,0:T(8,128)(2,1)S(1)}, bf16[128,512]{1,0:T(8,128)(2,1)}, u32[]{:S(2)}) copy-start(bf16[128,512]{1,0:T(8,128)(2,1)} %get-tuple-element.11) | copy-start | bytes 393220
  94.0 1.0 copy-start
  94.9 0.7 copy-start.3
  95.0 1.2 %copy-start.2 = (f32[2,512]{1,0:T(2,128)S(1)}, f32[2,512]{1,0:T(2,128)}, u32[]{:S(2)}) copy-start(f32[2,512]{1,0:T(2,128)} %get-tuple-element.14) | copy-start | bytes 12292

commit v3 on v2

--- a/solution.py
+++ b/solution.py
@@ -17,7 +17,9 @@
 CHUNKS = 8
 SPAN = BLOCK * CHUNKS
 HALF = 16
+MEMBERS = 2 * HALF
 SLOTS = 2
+NOTE = 5
 LINE = 4
 COLS = GROUP * HEAD_SIZE
 SCALE = 1.0 / math.sqrt(HEAD_SIZE)
@@ -82,9 +84,9 @@
     q_in, k_in, v_in, g_in,
     dq_out, dk_out, dv_out, qb_out, kvb_out,
     qs, gs, ks, vs, scores, dprobs, dqs, dkst, dvst, dqst, rk, rv, met,
-    notes, notes_in, over_groups, groups_in, over_halves, halves_in,
+    notes, notes_in, over_groups, groups_in,
     q_send, q_recv, k_send, k_recv, x_send, d_send, d_recv, m_send, m_recv, dq_send, dq_recv,
-    n_send, n_recv, g_send, g_recv, h_send, h_recv,
+    n_send, n_recv, g_send, g_recv,
 ):
     me = lax.axis_index("seq")
     group = lax.axis_index("dp")
@@ -95,17 +97,16 @@
     row = index // LINE
     column = chunk % 2
     beside = me + 2 - 4 * column
-    opposite = (me + HALF) % (2 * HALF)
+    above = me + LINE - MEMBERS * (me // (MEMBERS - LINE))
 
     barrier = pltpu.get_barrier_semaphore()
 
     def greet(device):
         pl.semaphore_signal(barrier, inc=1, device_id=device, device_id_type=MESH)
 
-    each(1, HALF, lambda i: greet({"seq": base + (index + i) % HALF}))
+    each(1, MEMBERS, lambda i: greet({"seq": (me + i) % MEMBERS}))
     each(1, groups, lambda i: greet({"dp": (group + i) % groups}))
-    greet({"seq": opposite})
-    pl.semaphore_wait(barrier, HALF - 1 + groups - 1 + 1)
+    pl.semaphore_wait(barrier, MEMBERS - 1 + groups - 1)
 
     def spread(act):
         for slot in range(SLOTS):
@@ -135,27 +136,39 @@
                             me,
                         )
 
-                each(0, LINE - row, lambda i: push(LINE - 1 - i, column, LINE - 1 - i))
+                push(row, column, 0)
+
+                @pl.when(row < LINE - 1)
+                def _():
+                    push(row + 1, column, 1)
 
                 @pl.when(column == 0)
                 def _():
-                    push(row, 1, LINE)
-
-    def across(slot, part, line, act):
-        place = (ks, vs)[part]
-        block = place.at[slot, at((2 * line + column) * BLOCK, BLOCK)]
+                    push(row, 1, 2)
+
+    def pass_on(slot, part, line, act):
+        block = (ks, vs)[part].at[slot, at((2 * line + column) * BLOCK, BLOCK)]
         sem = k_recv.at[slot, 2 * line + column, part]
         act(block, sem, x_send.at[slot, part, line])
 
     def hand_on(block, sem, out_sem):
         landed(block, sem)
-        remote(block, block, out_sem, sem, {"seq": beside}).start()
+
+        @pl.when(row < LINE - 1)
+        def _():
+            remote(block, block, out_sem.at[1], sem, {"seq": above}).start()
+
+        remote(block, block, out_sem.at[0], sem, {"seq": beside}).start()
 
     def handed_on(block, sem, out_sem):
-        remote(block, block, out_sem, sem, {"seq": beside}).wait_send()
+        @pl.when(row < LINE - 1)
+        def _():
+            remote(block, block, out_sem.at[1], sem, {"seq": above}).wait_send()
+
+        remote(block, block, out_sem.at[0], sem, {"seq": beside}).wait_send()
 
     spread(send)
-    each(0, row, lambda i: across(0, 0, row - 1 - i, hand_on))
+    each(0, row, lambda i: pass_on(0, 0, row - 1 - i, hand_on))
 
     first = 2 * row
     key_ids = lax.broadcasted_iota(jnp.int32, (BLOCK, BLOCK), 0)
@@ -235,10 +248,15 @@
                 line = row - 1 - i
                 wait_block(2 * line + 1 - column, part)
                 c = step(2 * line, 2, c, False)
+                if part == 0:
+
+                    @pl.when(slot == 1)
+                    def _():
+                        settle(0, line)
 
                 @pl.when(slot == 0)
                 def _():
-                    across(next_slot, next_part, line, hand_on)
+                    pass_on(next_slot, next_part, line, hand_on)
 
                 return c
 
@@ -303,15 +321,13 @@
 
             back_across(send, slot, line)
 
-            @pl.when(line > 0)
+            @pl.when(slot * line > 1)
             def _():
-                @pl.when(slot * (line - 1) == 0)
-                def _():
-                    settle(slot, line - 1)
+                settle(1, line - 2)
 
             @pl.when(slot == 0)
             def _():
-                across(1, 1, line, hand_on)
+                pass_on(1, 1, line, hand_on)
 
             return bias
 
@@ -321,44 +337,41 @@
 
         @pl.when(slot == 0)
         def _():
-            back_own(send, slot)
-
-            @pl.when(row > 0)
-            def _():
-                settle(slot, row - 1)
+            back_own(send, 0)
 
         for part in range(2):
-            notes[0, pl.ds(1 + 2 * slot + part, 1), :] = jnp.sum(bias[part], axis=0, keepdims=True)
+            notes[0, 1 + 2 * slot + part] = jnp.sum(bias[part], axis=0, keepdims=True)
         for j in range(GROUP):
             x = dqs[j] * SCALE
             x = x.T
             dqst[slot, :, cols[j]] = x.astype(BF16)
-            notes[slot * GROUP + j, pl.ds(0, 1), :] = jnp.sum(
-                fold(x, jnp.sum), axis=0, keepdims=True
-            )
+            notes[slot * GROUP + j, 0] = jnp.sum(fold(x, jnp.sum), axis=0, keepdims=True)
         return carry
 
     notes[...] = jnp.zeros_like(notes)
     lax.fori_loop(0, SLOTS, job, 0)
 
     for i in range(1, HALF):
-        notes[i, pl.ds(1, 4), :] = notes[0, pl.ds(1, 4), :]
+        for j in range(1, NOTE):
+            notes[i, j] = notes[0, j]
 
     def tell(i, act):
-        act(notes.at[i], notes_in.at[index], n_send.at[i], n_recv, base + i, me)
-
-    each(0, HALF, lambda i: tell(i, send))
+        act(notes.at[i % HALF], notes_in.at[me], n_send.at[i], n_recv, i, me)
+
+    each(0, MEMBERS, lambda i: tell(i, send))
     back_own(send, 1)
-    each(row // 2, row, lambda line: settle(1, line))
+    each(row // 3, row, lambda line: settle(1, line))
     for slot in range(SLOTS):
         back_rows(send, slot)
 
     landed(notes_in, n_recv)
     sums = [notes_in[0], notes_in[1]]
-    for i in range(2, HALF):
+    for i in range(2, MEMBERS):
         sums[i % 2] = sums[i % 2] + notes_in[i]
+    over_groups[0] = jnp.where(base == 0, sums[0][0], sums[1][0])
     for i in range(2):
-        over_groups[i] = sums[i]
+        for j in range(1, NOTE):
+            over_groups[i * (NOTE - 1) + j] = sums[i][j]
 
     def to_group(i):
         return remote(
@@ -367,18 +380,11 @@
 
     each(1, groups, lambda i: to_group(i).start())
     landed(groups_in, g_recv)
-    over_halves[...] = over_groups[...] + jnp.sum(groups_in[...], axis=0)
-    to_half = remote(over_halves, halves_in, h_send, h_recv, {"seq": opposite})
-    to_half.start()
-    to_half.wait_recv()
-    sums = (over_halves[...] + halves_in[...]) * norm
-    qb_out[...] = jnp.where(base == 0, sums[0, 0:1], sums[1, 0:1])
+    sums = (over_groups[...] + jnp.sum(groups_in[...], axis=0)) * norm
+    qb_out[...] = sums[0]
     for head in range(KEYVALUE_HEADS):
         for part in range(2):
-            at_row = 1 + 2 * (head % 2) + part
-            kvb_out[pl.ds(part, 1), pl.ds(head * HEAD_SIZE, HEAD_SIZE)] = sums[
-                head // 2, at_row : at_row + 1
-            ]
+            kvb_out[pl.ds(part, 1), pl.ds(head * HEAD_SIZE, HEAD_SIZE)] = sums[1 + 2 * head + part]
 
     for part in range(2):
         place, out = ((rk, dk_out), (rv, dv_out))[part]
@@ -395,24 +401,33 @@
     spread(sent)
     for slot in range(SLOTS):
         for part in range(2):
-            each(0, row, lambda line: across(slot, part, line, handed_on))
+            each(0, row, lambda line: pass_on(slot, part, line, handed_on))
         back_own(sent, slot)
         each(0, row, lambda line: back(sent, slot, 2 * line + column, row))
         each(0, row, lambda line: back_across(sent, slot, line))
         back_rows(sent, slot)
-    each(0, HALF, lambda i: tell(i, sent))
+    each(0, MEMBERS, lambda i: tell(i, sent))
     each(1, groups, lambda i: to_group(i).wait_send())
-    to_half.wait_send()
+
+
+def hand_out(*refs):
+    *refs, sems = refs
+    count = len(refs) // 2
+    copies = [pltpu.make_async_copy(refs[i], refs[count + i], sems.at[i]) for i in range(count)]
+    for copy in copies:
+        copy.start()
+    for copy in copies:
+        copy.wait()
 
 
 def local(query_input, key_input, value_input, output_gradient):
     groups = lax.axis_size("dp")
-    norm = 1.0 / math.sqrt(ROWS * 2 * HALF * groups)
+    norm = 1.0 / math.sqrt(ROWS * MEMBERS * groups)
     vmem = pl.BlockSpec(memory_space=pltpu.VMEM)
     any_space = pl.BlockSpec(memory_space=pl.ANY)
     dma = pltpu.SemaphoreType.DMA
     kv_cols = KEYVALUE_HEADS * HEAD_SIZE
-    return tuple(
+    results = tuple(
         pl.pallas_call(
             functools.partial(kernel, groups, norm),
             out_shape=[
@@ -438,28 +453,24 @@
                 pltpu.VMEM((LINE + 1, ROWS, kv_cols), BF16),
                 pltpu.VMEM((LINE + 1, ROWS, kv_cols), BF16),
                 pltpu.VMEM((SLOTS, 2, LINE - 1, BLOCK, HEAD_SIZE), BF16),
-                pltpu.VMEM((HALF, 8, HEAD_SIZE), F32),
-                pltpu.VMEM((HALF, 8, HEAD_SIZE), F32),
-                pltpu.VMEM((2, 8, HEAD_SIZE), F32),
-                pltpu.VMEM((groups - 1, 2, 8, HEAD_SIZE), F32),
-                pltpu.VMEM((2, 8, HEAD_SIZE), F32),
-                pltpu.VMEM((2, 8, HEAD_SIZE), F32),
+                pltpu.VMEM((HALF, NOTE, 1, HEAD_SIZE), F32),
+                pltpu.VMEM((MEMBERS, NOTE, 1, HEAD_SIZE), F32),
+                pltpu.VMEM((2 * NOTE - 1, 1, HEAD_SIZE), F32),
+                pltpu.VMEM((groups - 1, 2 * NOTE - 1, 1, HEAD_SIZE), F32),
                 dma((KEYVALUE_HEADS, 2)),
                 dma((SLOTS, 2)),
-                dma((LINE + 1, KEYVALUE_HEADS, 2)),
+                dma((3, KEYVALUE_HEADS, 2)),
                 dma((SLOTS, CHUNKS, 2)),
-                dma((SLOTS, 2, LINE)),
+                dma((SLOTS, 2, LINE - 1, 2)),
                 dma((SLOTS, CHUNKS, 2, 2)),
                 dma((LINE + 1, 2)),
                 dma((SLOTS, 2, LINE - 1)),
                 dma((SLOTS, 2, LINE - 1)),
                 dma((SLOTS, 2)),
                 dma,
-                dma((HALF,)),
+                dma((MEMBERS,)),
                 dma,
                 dma((groups - 1,)),
-                dma,
-                dma,
                 dma,
             ],
             compiler_params=pltpu.CompilerParams(
@@ -467,6 +478,16 @@
             ),
             name="attention_grads",
         )(query_input, key_input, value_input, output_gradient)
+    )
+    return tuple(
+        pl.pallas_call(
+            hand_out,
+            out_shape=[jax.ShapeDtypeStruct(x.shape, x.dtype) for x in results],
+            in_specs=[vmem] * len(results),
+            out_specs=[any_space] * len(results),
+            scratch_shapes=[dma((len(results),))],
+            name="hand_out",
+        )(*results)
     )
 
 

time: 97 us -> 87.4 us (0.901)
  local copies, waits for them, and re-layouts: 5.04 us -> 0 us
  Pallas kernels: 91 us -> 86.6 us
    pallas_call x1, Pallas kernels: 91 us -> 84.2 us  [local(): pl.pallas_call(functools.partial(kernel, groups, norm), out_shape=[jax.Sh...]
    unnamed x13 -> x0, local copies, waits for them, and re-layouts: 5.04 us -> none
    pallas_call x0 -> x1, Pallas kernels: none -> 2.4 us  [local(): pl.pallas_call(hand_out, out_shape=[jax.ShapeDtypeStruct(x.shape, x.dtype...]
where the time goes in v3:
time: 87.4 us; the launch traced here: 87.2 us
  Pallas kernels  86.6 us (99%)
    pallas_call x1, Pallas kernels, local(): pl.pallas_call(functools.partial(kernel, groups, norm), out_shape=[jax.Sh...  84.2 us
    pallas_call x1, Pallas kernels, local(): pl.pallas_call(hand_out, out_shape=[jax.ShapeDtypeStruct(x.shape, x.dtype...  2.4 us

profile of v3, /device:TPU:1, one launch (start us, length us, event | category | flops | bytes accessed | tf_op | source)
XLA Modules:
  0.0 87.2 jit_solution(70630473280306181)
XLA Ops:
  0.6 84.2 %attention_grads.1 = (bf16[128,4096]{1,0:T(8,128)(2,1)}, bf16[128,512]{1,0:T(8,128)(2,1)}, bf16[128,512]{1,0:T(8,128)(2,1)}, f32[1,128]{1,0:T(1,128)}, f32[2,512]{1,0:T(2,128)}) custom-call(bf16[128,4096]{1,0:T(8,128)(2,1)} %q_in.1, bf16[128,512]{1,0:T(8,128)(2,1)} %k_in.1, bf16[128,512]{1,0:T(8,128)(2,1)} %v_in.1, bf16[128,4096]{1,0:T(8,128)(2,1)} %g_in.1), custom_call_target="tpu_custom_call" | custom-call | tf_op jit(solution)/shard_map/attention_grads/pallas_call | solution.py:431
  84.8 2.4 %hand_out.1 = (bf16[128,4096]{1,0:T(8,128)(2,1)}, bf16[128,512]{1,0:T(8,128)(2,1)}, bf16[128,512]{1,0:T(8,128)(2,1)}, f32[1,128]{1,0:T(1,128)}, f32[2,512]{1,0:T(2,128)}) custom-call(bf16[128,4096]{1,0:T(8,128)(2,1)} %get-tuple-element.10.refs_0_, bf16[128,512]{1,0:T(8,128)(2,1)} %get-tuple-element.11.refs_1_, bf16[128,512]{1,0:T(8,128)(2,1)} %get-tuple-element.12.refs_2_, ...), custom_call_target="tpu_custom_call" | custom-call | tf_op jit(solution)/shard_map/hand_out/pallas_call | solution.py:483

commit v4 on v3

--- a/solution.py
+++ b/solution.py
@@ -113,17 +113,6 @@
             for part in range(2):
                 rows_in, rows_at = ((q_in, qs), (g_in, gs))[part]
                 keys_in, keys_at = ((k_in, ks), (v_in, vs))[part]
-                for to in range(2):
-                    head = 2 * to + slot
-                    act(
-                        rows_in.at[:, pl.ds(head * COLS, COLS)],
-                        rows_at.at[slot, at(core * ROWS, ROWS)],
-                        q_send.at[head, part],
-                        q_recv.at[slot, part],
-                        base + chunk * 2 + to,
-                        me,
-                    )
-
                 def push(line, there, lane):
                     for to in range(2):
                         head = 2 * to + slot
@@ -136,15 +125,26 @@
                             me,
                         )
 
-                push(row, column, 0)
-
                 @pl.when(row < LINE - 1)
                 def _():
                     push(row + 1, column, 1)
 
+                push(row, column, 0)
+
                 @pl.when(column == 0)
                 def _():
                     push(row, 1, 2)
+
+                for to in range(2):
+                    head = 2 * to + slot
+                    act(
+                        rows_in.at[:, pl.ds(head * COLS, COLS)],
+                        rows_at.at[slot, at(core * ROWS, ROWS)],
+                        q_send.at[head, part],
+                        q_recv.at[slot, part],
+                        base + chunk * 2 + to,
+                        me,
+                    )
 
     def pass_on(slot, part, line, act):
         block = (ks, vs)[part].at[slot, at((2 * line + column) * BLOCK, BLOCK)]
@@ -168,7 +168,12 @@
         remote(block, block, out_sem.at[0], sem, {"seq": beside}).wait_send()
 
     spread(send)
-    each(0, row, lambda i: pass_on(0, 0, row - 1 - i, hand_on))
+    top = row // (LINE - 1)
+
+    def first_keys(count):
+        each(0, count, lambda i: pass_on(0, 0, row - 1 - i, hand_on))
+
+    first_keys(row * (1 - top))
 
     first = 2 * row
     key_ids = lax.broadcasted_iota(jnp.int32, (BLOCK, BLOCK), 0)
@@ -236,13 +241,18 @@
 
         def walk(step, part, carry, next_slot, next_part):
             wait_block(chunk, part)
-            carry = step(chunk, 1, carry, True)
-
-            def partner(i, c):
+
+            def both(i, c):
                 wait_block(first, part)
-                return step(first, 1, c, False)
-
-            carry = lax.fori_loop(0, column, partner, carry)
+                return step(first, 2, c, True)
+
+            carry = lax.fori_loop(0, column, both, carry)
+            carry = lax.fori_loop(0, 1 - column, lambda i, c: step(first, 1, c, True), carry)
+            if part == 0:
+
+                @pl.when(slot == 0)
+                def _():
+                    first_keys(row * top)
 
             def below(i, c):
                 line = row - 1 - i
@@ -269,7 +279,9 @@
             for j in range(GROUP):
                 s = dot(key_block, qs[slot, :, cols[j]], NT)
                 if diagonal:
-                    s = jnp.where(key_ids <= query_ids, s, -jnp.inf)
+                    edge = (size - 1) * BLOCK
+                    tail = jnp.where(key_ids <= query_ids, s[edge:], -jnp.inf)
+                    s = jnp.concatenate([s[:edge], tail], axis=0) if edge else tail
                 scores[j, rows, :] = s
                 out.append(jnp.maximum(peaks[j], fold(s, jnp.max)))
             return tuple(out)
@@ -333,7 +345,8 @@
 
         zero = jnp.zeros((8, HEAD_SIZE), F32)
         bias = lax.fori_loop(0, row, grads_below, (zero, zero))
-        bias = lax.fori_loop(first, chunk + 1, lambda b, c: pass_grads(b, 1, c), bias)
+        bias = lax.fori_loop(0, column, lambda i, c: pass_grads(first, 2, c), bias)
+        bias = lax.fori_loop(0, 1 - column, lambda i, c: pass_grads(first, 1, c), bias)
 
         @pl.when(slot == 0)
         def _():
@@ -346,6 +359,11 @@
             x = x.T
             dqst[slot, :, cols[j]] = x.astype(BF16)
             notes[slot * GROUP + j, 0] = jnp.sum(fold(x, jnp.sum), axis=0, keepdims=True)
+
+        @pl.when(slot == 0)
+        def _():
+            back_rows(send, 0)
+
         return carry
 
     notes[...] = jnp.zeros_like(notes)
@@ -361,8 +379,19 @@
     each(0, MEMBERS, lambda i: tell(i, send))
     back_own(send, 1)
     each(row // 3, row, lambda line: settle(1, line))
+    back_rows(send, 1)
+
+    def back_all(slot):
+        back_own(sent, slot)
+        each(0, row, lambda line: back(sent, slot, 2 * line + column, row))
+        each(0, row, lambda line: back_across(sent, slot, line))
+        back_rows(sent, slot)
+
+    spread(sent)
     for slot in range(SLOTS):
-        back_rows(send, slot)
+        for part in range(2):
+            each(0, row, lambda line: pass_on(slot, part, line, handed_on))
+    back_all(0)
 
     landed(notes_in, n_recv)
     sums = [notes_in[0], notes_in[1]]
@@ -379,6 +408,7 @@
         )
 
     each(1, groups, lambda i: to_group(i).start())
+    each(0, MEMBERS, lambda i: tell(i, sent))
     landed(groups_in, g_recv)
     sums = (over_groups[...] + jnp.sum(groups_in[...], axis=0)) * norm
     qb_out[...] = sums[0]
@@ -398,15 +428,7 @@
 
     landed(dq_out, dq_recv)
 
-    spread(sent)
-    for slot in range(SLOTS):
-        for part in range(2):
-            each(0, row, lambda line: pass_on(slot, part, line, handed_on))
-        back_own(sent, slot)
-        each(0, row, lambda line: back(sent, slot, 2 * line + column, row))
-        each(0, row, lambda line: back_across(sent, slot, line))
-        back_rows(sent, slot)
-    each(0, MEMBERS, lambda i: tell(i, sent))
+    back_all(1)
     each(1, groups, lambda i: to_group(i).wait_send())
 
 

time: 87.4 us -> 86.8 us (level)
  no operation moved by 1% of the time
where the time goes in v4:
time: 86.8 us; the launch traced here: 86.6 us
  Pallas kernels  86 us (99%)
    pallas_call x1, Pallas kernels, local(): pl.pallas_call(functools.partial(kernel, groups, norm), out_shape=[jax.Sh...  83.5 us
    pallas_call x1, Pallas kernels, local(): pl.pallas_call(hand_out, out_shape=[jax.ShapeDtypeStruct(x.shape, x.dtype...  2.4 us

profile of v4, /device:TPU:1, one launch (start us, length us, event | category | flops | bytes accessed | tf_op | source)
XLA Modules:
  0.0 86.6 jit_solution(2146607077753649608)
XLA Ops:
  0.6 83.5 %attention_grads.1 = (bf16[128,4096]{1,0:T(8,128)(2,1)}, bf16[128,512]{1,0:T(8,128)(2,1)}, bf16[128,512]{1,0:T(8,128)(2,1)}, f32[1,128]{1,0:T(1,128)}, f32[2,512]{1,0:T(2,128)}) custom-call(bf16[128,4096]{1,0:T(8,128)(2,1)} %q_in.1, bf16[128,512]{1,0:T(8,128)(2,1)} %k_in.1, bf16[128,512]{1,0:T(8,128)(2,1)} %v_in.1, bf16[128,4096]{1,0:T(8,128)(2,1)} %g_in.1), custom_call_target="tpu_custom_call" | custom-call | tf_op jit(solution)/shard_map/attention_grads/pallas_call | solution.py:453
  84.2 2.4 %hand_out.1 = (bf16[128,4096]{1,0:T(8,128)(2,1)}, bf16[128,512]{1,0:T(8,128)(2,1)}, bf16[128,512]{1,0:T(8,128)(2,1)}, f32[1,128]{1,0:T(1,128)}, f32[2,512]{1,0:T(2,128)}) custom-call(bf16[128,4096]{1,0:T(8,128)(2,1)} %get-tuple-element.10.refs_0_, bf16[128,512]{1,0:T(8,128)(2,1)} %get-tuple-element.11.refs_1_, bf16[128,512]{1,0:T(8,128)(2,1)} %get-tuple-element.12.refs_2_, ...), custom_call_target="tpu_custom_call" | custom-call | tf_op jit(solution)/shard_map/hand_out/pallas_call | solution.py:505
